TPU v7x, 512 devices: a whole 4x8x8 slice. The times are simulated.
512 devices in a mesh: ep: 64 (over z, y), tp: 8 (over x, core).
Axes of the slice: x: 4, y: 8, z: 8, core: 2. Of those that a mesh axis runs over, the one named last changes fastest.
Arguments:
- tokens: bfloat16 [1024, 3072], P('ep'), may hold values from -6 to 6
- expert_ids: int32 [1024, 2], P('ep'), may hold values from 0 to 7, all different within a row; in each aligned block of 16 rows (0 to 15, 16 to 31, ...) at most 6 rows name the same one
- combine: float32 [1024, 2], P('ep'), may hold values from 0.2 to 1
- grad_out: bfloat16 [1024, 3072], P('ep'), may hold values from -6 to 6
- gate_weight: bfloat16 [3072, 65536], P(None, ('ep', 'tp')), may hold values from -0.109375 to 0.109375
- up_weight: bfloat16 [3072, 65536], P(None, ('ep', 'tp')), may hold values from -0.109375 to 0.109375
- down_weight: bfloat16 [65536, 3072], P(('ep', 'tp')), may hold values from -0.0625 to 0.0625
Outputs:
- mixed: bfloat16 [1024, 3072], P('ep')
- grad_tokens: bfloat16 [1024, 3072], P('ep')
- grad_combine: float32 [1024, 2], P('ep')
- grad_gate: bfloat16 [3072, 65536], P(None, ('ep', 'tp'))
- grad_up: bfloat16 [3072, 65536], P(None, ('ep', 'tp'))
- grad_down: bfloat16 [65536, 3072], P(('ep', 'tp'))
Inputs may be any that keep to these rules, and one draw needn't show every extreme that they name: `expert_ids`: each row names 2 different experts. Among the 16 rows of one index of ep no expert is named more than 6 times, a bound that some block reaches.
All inputs are finite; a program needn't handle non-finite values.
Results may differ from a plain program's by a relative error of at most 0.0057.
Values may be sent and summed in bfloat16 or wider, within the bound.
A program may use at most 128 MiB of HBM per device.

v0:
```python
import jax
import jax.numpy as jnp
from jax import lax
from jax.sharding import PartitionSpec as P

E = 8
CAP = 6


def expert_rows(rows_in, rows_grad, gate_part, up_part, down_part):
    gate_pre = jnp.dot(rows_in, gate_part, preferred_element_type=jnp.float32)
    up_pre = jnp.dot(rows_in, up_part, preferred_element_type=jnp.float32)
    sigmoid_gate = jax.nn.sigmoid(gate_pre)
    silu_gate = gate_pre * sigmoid_gate
    hidden = (silu_gate * up_pre).astype(jnp.bfloat16)
    partial_value = jnp.dot(hidden, down_part, preferred_element_type=jnp.float32)
    d_hidden = lax.dot_general(
        rows_grad, down_part, (((1,), (1,)), ((), ())), preferred_element_type=jnp.float32
    )
    d_gate = (d_hidden * up_pre * sigmoid_gate * (1.0 + gate_pre * (1.0 - sigmoid_gate))).astype(
        jnp.bfloat16
    )
    d_up = (d_hidden * silu_gate).astype(jnp.bfloat16)
    back_rows = lax.dot_general(
        d_gate, gate_part, (((1,), (1,)), ((), ())), preferred_element_type=jnp.float32
    )
    back_rows = back_rows + lax.dot_general(
        d_up, up_part, (((1,), (1,)), ((), ())), preferred_element_type=jnp.float32
    )
    grad_down = lax.dot_general(
        hidden, rows_grad, (((0,), (0,)), ((), ())), preferred_element_type=jnp.float32
    )
    grad_gate = lax.dot_general(
        rows_in, d_gate, (((0,), (0,)), ((), ())), preferred_element_type=jnp.float32
    )
    grad_up = lax.dot_general(
        rows_in, d_up, (((0,), (0,)), ((), ())), preferred_element_type=jnp.float32
    )
    return (partial_value, back_rows, grad_gate, grad_up, grad_down)


def body(tokens, expert_ids, combine, grad_out, gate_weight, up_weight, down_weight):
    tok_dev, width = tokens.shape
    top_count = expert_ids.shape[1]
    assigned = tok_dev * top_count
    n_ep = lax.axis_size("ep")
    group_size = n_ep // E
    capacity = CAP
    flat_ids = expert_ids.reshape(assigned)
    onehot = (flat_ids[:, None] == jnp.arange(E, dtype=jnp.int32)[None, :]).astype(jnp.int32)
    rank_in = jnp.sum((jnp.cumsum(onehot, axis=0) - 1) * onehot, axis=1)
    slot_id = flat_ids * capacity + rank_in
    picker = jnp.arange(E * capacity, dtype=jnp.int32)[:, None] == slot_id[None, :]
    picker_half = picker.astype(jnp.bfloat16)
    picker_full = picker.astype(jnp.float32)
    tokens_rep = jnp.repeat(tokens, top_count, axis=0)
    scaled = (
        combine.reshape(assigned)[:, None]
        * jnp.repeat(grad_out, top_count, axis=0).astype(jnp.float32)
    ).astype(jnp.bfloat16)
    picked_in = jnp.dot(picker_half, tokens_rep, preferred_element_type=jnp.float32).astype(
        jnp.bfloat16
    )
    picked_grad = jnp.dot(picker_half, scaled, preferred_element_type=jnp.float32).astype(
        jnp.bfloat16
    )

    def spread(values):
        span = values.shape[1]
        shaped = values.reshape(E, 1, capacity, span)
        return jnp.broadcast_to(shaped, (E, group_size, capacity, span)).reshape(
            n_ep * capacity, span
        )

    rows_in, rows_grad = (
        lax.all_to_all(spread(picked_in), "ep", split_axis=0, concat_axis=0, tiled=True),
        lax.all_to_all(spread(picked_grad), "ep", split_axis=0, concat_axis=0, tiled=True),
    )
    partial_value, back_rows, grad_g, grad_u, grad_d = expert_rows(
        rows_in, rows_grad, gate_weight, up_weight, down_weight
    )

    def collect(values):
        span = values.shape[1]
        summed = jnp.sum(values.reshape(E, group_size, capacity, span), axis=1).reshape(
            E * capacity, span
        )
        chosen = lax.dot_general(
            picker_full,
            summed,
            (((0,), (0,)), ((), ())),
            precision=lax.Precision.HIGHEST,
            preferred_element_type=jnp.float32,
        )
        return chosen.reshape(tok_dev, top_count, span)

    returned_out, returned_back = (
        lax.all_to_all(partial_value, "ep", split_axis=0, concat_axis=0, tiled=True),
        lax.all_to_all(back_rows, "ep", split_axis=0, concat_axis=0, tiled=True),
    )
    expert_out = collect(returned_out)
    back_all = collect(returned_back)
    mixed_part = jnp.sum(combine[:, :, None] * expert_out, axis=1)
    grad_tok_part = jnp.sum(back_all, axis=1)
    score_part = jnp.sum(grad_out.astype(jnp.float32)[:, None, :] * expert_out, axis=2)
    mixed_sum, grad_tok_sum, grad_combine = lax.psum((mixed_part, grad_tok_part, score_part), "tp")
    mixed = mixed_sum.astype(jnp.bfloat16)
    grad_tokens = grad_tok_sum.astype(jnp.bfloat16)
    return (
        mixed,
        grad_tokens,
        grad_combine,
        grad_g.astype(jnp.bfloat16),
        grad_u.astype(jnp.bfloat16),
        grad_d.astype(jnp.bfloat16),
    )


def solution(mesh):
    return jax.shard_map(
        body,
        mesh=mesh,
        in_specs=(
            P("ep", None),
            P("ep", None),
            P("ep", None),
            P("ep", None),
            P(None, ("ep", "tp")),
            P(None, ("ep", "tp")),
            P(("ep", "tp"), None),
        ),
        out_specs=(
            P("ep", None),
            P("ep", None),
            P("ep", None),
            P(None, ("ep", "tp")),
            P(None, ("ep", "tp")),
            P(("ep", "tp"), None),
        ),
        check_vma=False,
    )
```

profile of v0, /device:TPU:112, one launch (start us, length us, event | category | flops | bytes accessed | tf_op | source)
XLA Modules:
  0.0 682.5 jit_solution(16639735246712941525)
XLA Ops:
  0.6 0.0 copy-start
  0.6 0.8 copy.15
  1.5 0.1 reshape.102
  1.6 0.1 fusion.2
  1.6 0.1 reduce_window_sum.11
  1.7 0.2 select_reduce_fusion
  1.9 1.0 broadcast_in_dim.12
  2.9 0.1 reshape.103
  3.0 0.2 convolution_convert_fusion.4
  3.2 0.1 broadcast_in_dim.26
  3.3 2.1 broadcast_in_dim.27
  5.4 0.0 copy-start.9
  5.4 0.0 copy-start.5
  5.4 15.4 %all-to-all-start = ((bf16[64,6,3072]{2,1,0:T(8,128)(2,1)}), bf16[64,6,3072]{2,1,0:T(8,128)(2,1)}, u32[]{:S(2)}, u32[]{:S(2)}) async-start(bf16[64,6,3072]{2,1,0:T(8,128)(2,1)} %bitcast.27), calls=%async_computation | async-start | bytes 6291456 | tf_op jit(solution)/shard_map/all_to_all | solution.py:76
  20.8 0.0 copy-done.9
  20.8 0.1 copy.17
  20.9 0.1 mul.65
  21.0 0.0 copy-done.5
  21.0 0.1 broadcast_in_dim.28.clone
  21.1 0.3 convert_element_type.51
  21.4 0.3 convolution_convert_fusion.3
  21.7 0.1 broadcast_in_dim.29
  21.8 92.0 %all-to-all-done = bf16[64,6,3072]{2,1,0:T(8,128)(2,1)} async-done(((bf16[64,6,3072]{2,1,0:T(8,128)(2,1)}), bf16[64,6,3072]{2,1,0:T(8,128)(2,1)}, u32[]{:S(2)}, u32[]{:S(2)}) %all-to-all-start) | async-done | bytes 2359328 | tf_op jit(solution)/shard_map/all_to_all | solution.py:76
  113.8 2.1 broadcast_in_dim.30
  115.9 9.2 %all-to-all-start.2 = ((bf16[64,6,3072]{2,1,0:T(8,128)(2,1)}), bf16[64,6,3072]{2,1,0:T(8,128)(2,1)}, u32[]{:S(2)}, u32[]{:S(2)}) async-start(bf16[64,6,3072]{2,1,0:T(8,128)(2,1)} %bitcast.28), calls=%async_computation.2 | async-start | bytes 6291456 | tf_op jit(solution)/shard_map/all_to_all | solution.py:77
  125.1 3.0 all_to_all.30
  128.1 0.0 copy-start.3
  128.1 2.7 fusion.9
  130.8 0.0 copy-done.3
  130.8 1.5 fusion.8
  132.2 84.5 %all-to-all-done.2 = bf16[64,6,3072]{2,1,0:T(8,128)(2,1)} async-done(((bf16[64,6,3072]{2,1,0:T(8,128)(2,1)}), bf16[64,6,3072]{2,1,0:T(8,128)(2,1)}, u32[]{:S(2)}, u32[]{:S(2)}) %all-to-all-start.2) | async-done | bytes 2359328 | tf_op jit(solution)/shard_map/all_to_all | solution.py:77
  216.7 4.4 all_to_all.35
  221.1 0.0 copy-done
  221.1 0.0 copy-start.4
  221.1 2.6 multiply_convert_fusion.2
  223.7 0.0 copy-start.7
  223.8 0.0 copy-done.4
  223.8 0.0 copy-start.2
  223.8 0.8 fusion.11
  224.6 0.0 copy-done.7
  224.6 0.4 copy-done.2
  224.9 2.9 convolution_add_fusion
  227.9 5.6 all_to_all.36
  233.5 7.6 %all-to-all-start.3 = ((f32[64,6,3072]{2,1,0:T(8,128)}), f32[64,6,3072]{2,1,0:T(8,128)}, u32[]{:S(2)}, u32[]{:S(2)}) async-start(f32[64,6,3072]{2,1,0:T(8,128)} %all_to_all.36), calls=%async_computation.3 | async-start | bytes 12582912 | tf_op jit(solution)/shard_map/all_to_all | solution.py:99
  241.0 2.9 fusion.10
  244.0 5.5 all_to_all.31
  249.5 0.0 copy-start.6
  249.5 180.1 %all-to-all-done.3 = f32[64,6,3072]{2,1,0:T(8,128)} async-done(((f32[64,6,3072]{2,1,0:T(8,128)}), f32[64,6,3072]{2,1,0:T(8,128)}, u32[]{:S(2)}, u32[]{:S(2)}) %all-to-all-start.3) | async-done | bytes 4718624 | tf_op jit(solution)/shard_map/all_to_all | solution.py:99
  429.6 9.0 %all-to-all-start.1 = ((f32[64,6,3072]{2,1,0:T(8,128)}), f32[64,6,3072]{2,1,0:T(8,128)}, u32[]{:S(2)}, u32[]{:S(2)}) async-start(f32[64,6,3072]{2,1,0:T(8,128)} %all_to_all.31), calls=%async_computation.1 | async-start | bytes 12582912 | tf_op jit(solution)/shard_map/all_to_all | solution.py:98
  438.6 0.0 copy-done.6
  438.6 0.1 iota_compare_fusion.4
  438.7 3.2 convolution_convert_fusion
  441.9 1.7 convolution_convert_fusion.1
  443.6 0.0 copy-done.8
  443.6 1.7 convolution_convert_fusion.2
  445.3 3.3 bitcast_reduce_fusion
  448.5 0.1 reshape.109
  448.6 0.4 convolution_reduce_fusion
  449.0 177.2 %all-to-all-done.1 = f32[64,6,3072]{2,1,0:T(8,128)} async-done(((f32[64,6,3072]{2,1,0:T(8,128)}), f32[64,6,3072]{2,1,0:T(8,128)}, u32[]{:S(2)}, u32[]{:S(2)}) %all-to-all-start.1) | async-done | bytes 4718624 | tf_op jit(solution)/shard_map/all_to_all | solution.py:98
  626.2 3.3 bitcast_reduce_fusion.1
  629.5 0.1 reshape.108
  629.6 0.5 multiply_reduce_fusion
  630.1 52.4 %all-reduce.2 = (bf16[16,3072]{1,0:T(8,128)(2,1)}, bf16[16,3072]{1,0:T(8,128)(2,1)}, f32[16,2]{0,1:T(2,128)}) all-reduce(f32[16,3072]{1,0:T(8,128)S(1)} %get-tuple-element.7, f32[16,3072]{1,0:T(8,128)S(1)} %convolution_reduce_fusion, f32[16,2]{0,1:T(2,128)S(1)} %get-tuple-element.6), channel_id=1, replica_groups=mesh['ep'=64,'tp'=8] {'tp'}, use_global_device_ids=true, to_apply=%region_4.5 | all-reduce | flops 98336 | bytes 590080 | tf_op jit(solution)/shard_map/psum | solution.py:106
  682.5 0.0 copy-done.1
  (5 shorter events, 0.0 us)
Async XLA Ops:
  0.6 220.5 %copy-start = (bf16[128,3072]{1,0:T(8,128)(2,1)S(1)}, bf16[128,3072]{1,0:T(8,128)(2,1)}, u32[]{:S(2)}) copy-start(bf16[128,3072]{1,0:T(8,128)(2,1)} %param.13) | copy-start | bytes 2359300
  5.4 15.4 %copy-start.9 = (f32[16,2]{0,1:T(2,128)S(1)}, f32[16,2]{0,1:T(2,128)}, u32[]{:S(2)}) copy-start(f32[16,2]{0,1:T(2,128)} %param.9) | copy-start | bytes 388
  5.4 15.6 %copy-start.5 = (bf16[16,3072]{1,0:T(8,128)(2,1)S(1)}, bf16[16,3072]{1,0:T(8,128)(2,1)}, u32[]{:S(2)}) copy-start(bf16[16,3072]{1,0:T(8,128)(2,1)} %param.10) | copy-start | bytes 294916
  5.4 108.4 %all-to-all-start = ((bf16[64,6,3072]{2,1,0:T(8,128)(2,1)}), bf16[64,6,3072]{2,1,0:T(8,128)(2,1)}, u32[]{:S(2)}, u32[]{:S(2)}) async-start(bf16[64,6,3072]{2,1,0:T(8,128)(2,1)} %bitcast.27), calls=%async_computation | async-start | bytes 6291456 | tf_op jit(solution)/shard_map/all_to_all | solution.py:76
  115.9 100.8 %all-to-all-start.2 = ((bf16[64,6,3072]{2,1,0:T(8,128)(2,1)}), bf16[64,6,3072]{2,1,0:T(8,128)(2,1)}, u32[]{:S(2)}, u32[]{:S(2)}) async-start(bf16[64,6,3072]{2,1,0:T(8,128)(2,1)} %bitcast.28), calls=%async_computation.2 | async-start | bytes 6291456 | tf_op jit(solution)/shard_map/all_to_all | solution.py:77
  128.1 2.7 copy-start.3
  221.1 2.6 copy-start.4
  223.7 0.8 copy-start.7
  223.8 1.2 copy-start.2
  233.5 196.1 %all-to-all-start.3 = ((f32[64,6,3072]{2,1,0:T(8,128)}), f32[64,6,3072]{2,1,0:T(8,128)}, u32[]{:S(2)}, u32[]{:S(2)}) async-start(f32[64,6,3072]{2,1,0:T(8,128)} %all_to_all.36), calls=%async_computation.3 | async-start | bytes 12582912 | tf_op jit(solution)/shard_map/all_to_all | solution.py:99
  249.5 189.1 %copy-start.6 = (bf16[16,3072]{1,0:T(8,128)(2,1)S(1)}, bf16[16,3072]{1,0:T(8,128)(2,1)}, u32[]{:S(2)}) copy-start(bf16[16,3072]{1,0:T(8,128)(2,1)} %param.10) | copy-start | bytes 294916
  429.6 196.6 %all-to-all-start.1 = ((f32[64,6,3072]{2,1,0:T(8,128)}), f32[64,6,3072]{2,1,0:T(8,128)}, u32[]{:S(2)}, u32[]{:S(2)}) async-start(f32[64,6,3072]{2,1,0:T(8,128)} %all_to_all.31), calls=%async_computation.1 | async-start | bytes 12582912 | tf_op jit(solution)/shard_map/all_to_all | solution.py:98
  441.9 1.7 copy-start.8
  626.2 56.3 %copy-start.1 = (bf16[128,3072]{1,0:T(8,128)(2,1)S(1)}, bf16[128,3072]{1,0:T(8,128)(2,1)}, u32[]{:S(2)}) copy-start(bf16[128,3072]{1,0:T(8,128)(2,1)} %param.13) | copy-start | bytes 2359300
where the time goes:
time: 683 us; the launch traced here: 682 us
  waiting for transfers between devices  534 us (78%)
  blocking collectives  52.4 us (8%)
  starting transfers between devices  41.2 us (6%)
  local copies, waits for them, and re-layouts  26.1 us (4%)
  matrix products  21.2 us (3%)
  other arithmetic  6.98 us (1%)
    all_to_all x1, waiting for transfers between devices, body(): lax.all_to_all(back_rows, 'ep', split_axis=0, concat_axis=0, tiled=True)  180 us
    all_to_all x1, waiting for transfers between devices, body(): lax.all_to_all(partial_value, 'ep', split_axis=0, concat_axis=0, tiled=True)  177 us
    all_to_all x1, waiting for transfers between devices, body(): lax.all_to_all(spread(picked_in), 'ep', split_axis=0, concat_axis=0, tile...  92 us
    all_to_all x1, waiting for transfers between devices, body(): lax.all_to_all(spread(picked_grad), 'ep', split_axis=0, concat_axis=0, ti...  84.5 us
    psum x1, blocking collectives, body(): lax.psum((mixed_part, grad_tok_part, score_part), 'tp')  52.4 us
    all_to_all x1, starting transfers between devices, body(): lax.all_to_all(spread(picked_in), 'ep', split_axis=0, concat_axis=0, tile...  15.4 us
  transfers between devices with their start and end apart: 4, of which 4 were waited for; matrix products, arithmetic and copies ran while one was open for 3% of the time, Pallas kernels for 0%

commit v1 on v0

v1 whole, which is shorter than its diff:
```python
import functools

import jax
import jax.numpy as jnp
from jax import lax
from jax.experimental import pallas as pl
from jax.experimental.pallas import tpu as pltpu
from jax.sharding import PartitionSpec as P

CAP = 6
CORES = 2
MESH = pl.DeviceIdType.MESH
F32 = jnp.float32
BF16 = jnp.bfloat16


def dot_nn(a, b):
    return jnp.dot(a, b, preferred_element_type=F32)


def dot_nt(a, b):
    return lax.dot_general(a, b, (((1,), (1,)), ((), ())), preferred_element_type=F32)


def dot_tn(a, b):
    return lax.dot_general(a, b, (((0,), (0,)), ((), ())), preferred_element_type=F32)


def kernel(
    dims,
    ids_ref, comb_ref, tok_ref, go_ref, gate_hbm, up_hbm, down_hbm,
    mixed_ref, gtok_ref, gcomb_ref, gg_hbm, gu_hbm, gd_hbm,
    xg, part, sib_out, sib_in, xs, xr, ys, yr, res,
    slab_out, slab_in, fin, fsc, pick, wgu, wd, hid, dgu, ggs, gus, gds,
    w_sem, za_s, za_r, zb_s, zb_r, gx, gy, g_send, d_send, d_recv,
    p_send, p_recv, rx_s, rx_r, ry_s, ry_r, f_s, f_r, o_sem,
):
    NX, NY, NZ, CAPA = dims
    PIECE = NZ * CAPA
    TOKB, D = tok_ref.shape
    SL = D // NX
    HS = SL // 2
    ROWS = NY * PIECE
    PER = NX * NY
    HID = wd.shape[1]

    ep, tp = lax.axis_index("ep"), lax.axis_index("tp")
    c, x = lax.rem(tp, CORES), lax.div(tp, CORES)
    y, z = lax.rem(ep, NY), lax.div(ep, NY)

    def wx(v):
        return lax.rem(v + 2 * NX, NX)

    def wy(v):
        return lax.rem(v + 2 * NY, NY)

    def at(xx, yy, zz, cc):
        return (zz * NY + yy, xx * CORES + cc)

    right, left = at(wx(x + 1), y, z, c), at(wx(x - 1), y, z, c)
    yup, ydown = at(x, wy(y + 1), z, c), at(x, wy(y - 1), z, c)
    sibling = at(x, y, z, 1 - c)
    xdev, ydev = (right, left), (yup, ydown)

    def remote(src, dst, ssem, rsem, device):
        return pltpu.make_async_remote_copy(
            src_ref=src, dst_ref=dst, send_sem=ssem, recv_sem=rsem,
            device_id=device, device_id_type=MESH,
        )

    def arrived(dst, rsem):
        remote(dst, dst, rsem, rsem, sibling).wait_recv()

    def sent(src, ssem):
        remote(src, src, ssem, ssem, sibling).wait_send()

    loads = []
    for i in range(NX):
        rows = pl.ds(i * SL, SL)
        loads.append(pltpu.make_async_copy(gate_hbm.at[rows, :], wgu.at[i, :, pl.ds(0, HID)], w_sem.at[3 * i]))
        loads.append(pltpu.make_async_copy(up_hbm.at[rows, :], wgu.at[i, :, pl.ds(HID, HID)], w_sem.at[3 * i + 1]))
        loads.append(pltpu.make_async_copy(down_hbm.at[:, rows], wd.at[i], w_sem.at[3 * i + 2]))
    for load in loads:
        load.start()

    barrier = pltpu.get_barrier_semaphore()
    peers_z = [at(x, y, lax.rem(z + d, NZ), c) for d in range(1, NZ)]
    NT = NX * CORES
    peers_t = [(ep, lax.rem(tp + d, NT)) for d in range(1, NT)]
    partners = peers_z + peers_t + [yup, ydown]
    for device in partners:
        pl.semaphore_signal(barrier, inc=1, device_id=device, device_id_type=MESH)

    lane = lax.broadcasted_iota(jnp.int32, (TOKB, NZ * 16), 1)
    expert, place = lax.shift_right_logical(lane, 4), lane & 15
    id0, id1 = ids_ref[:, 0:1], ids_ref[:, 1:2]
    is0, is1 = id0 == expert, id1 == expert
    named = jnp.where(is0 | is1, 1.0, 0.0)
    earlier = jnp.where(
        lax.broadcasted_iota(jnp.int32, (TOKB, TOKB), 0) > lax.broadcasted_iota(jnp.int32, (TOKB, TOKB), 1), 1.0, 0.0
    )
    rank = dot_nn(earlier.astype(BF16), named.astype(BF16)).astype(jnp.int32)
    hit0 = rank == place
    hit1 = (rank + CAPA == place) & (rank < CAPA)
    hit0 = hit0 & (place < CAPA)
    for g, mask in enumerate((is0 & hit0, is1 & hit0, is0 & hit1, is1 & hit1)):
        pick[g * TOKB : (g + 1) * TOKB, :] = jnp.where(mask, 1.0, 0.0).astype(BF16)

    one = jnp.ones((TOKB, 1), F32)
    w0 = jnp.where(c == 0, one, comb_ref[:, 0:1])
    w1 = jnp.where(c == 0, one, comb_ref[:, 1:2])
    span0 = pl.ds(pl.multiple_of(x * SL, 128), HS)
    span1 = pl.ds(pl.multiple_of(x * SL + HS, 128), HS)
    sources = []
    for span in (span0, span1):
        v = jnp.where(c == 0, tok_ref[:, span].astype(F32), go_ref[:, span].astype(F32))
        sources += [(v * w0).astype(BF16), (v * w1).astype(BF16)]
    slabs = dot_tn(pick[...], jnp.concatenate(sources, axis=0)).astype(BF16)
    for e in range(NZ):
        slab_out[0, e] = slabs[e * 16 : (e + 1) * 16]
    slab_in[0, z] = slab_out[0, z]

    pl.semaphore_wait(barrier, len(partners))

    def exchange_z(which, s_sem, r_sem):
        for d in range(1, NZ):
            remote(
                slab_out.at[which, lax.rem(z + d, NZ)], slab_in.at[which, z],
                s_sem.at[d], r_sem.at[d], peers_z[d - 1],
            ).start()
        for d in range(1, NZ):
            arrived(slab_in.at[which, lax.rem(z - d + NZ, NZ)], r_sem.at[d])

    exchange_z(0, za_s, za_r)

    row = lax.broadcasted_iota(jnp.int32, (PIECE, NZ * 16), 0)
    col = lax.broadcasted_iota(jnp.int32, (PIECE, NZ * 16), 1)
    block, inner = lax.shift_right_logical(col, 4), col & 15
    tidy0 = jnp.where((block * CAPA + inner == row) & (inner < CAPA), 1.0, 0.0).astype(BF16)
    tidy1 = jnp.where(
        (block * CAPA + inner - CAPA == row) & (inner >= CAPA) & (inner < 2 * CAPA), 1.0, 0.0
    ).astype(BF16)
    got = slab_in[0].reshape(NZ * 16, HS)
    mine = c * PER + x * NY + y
    xg[mine, :, 0:HS] = dot_nn(tidy0, got).astype(BF16)
    xg[mine, :, HS:SL] = dot_nn(tidy1, got).astype(BF16)

    halves = (pl.ds(0, HS), pl.ds(HS, HS))
    HX, HY = NX // 2, NY // 2

    def to_sibling(p):
        remote(xg.at[p], xg.at[p], d_send, d_recv, sibling).start()

    def send(ref, sem, device):
        remote(ref, ref, g_send, sem, device).start()

    def gather_y_then_x():
        def piece(xx, yy):
            return xx * NY + yy

        order = [0]
        for k in range(1, HY):
            order += [-k, k]
        order += [HY]

        def along_x(i):
            p = piece(x, wy(y + order[i]))
            send(xg.at[p], gx.at[0, i, 0], right)
            send(xg.at[p], gx.at[1, i, 0], left)
            to_sibling(p)

        def onward_x(i):
            yy = wy(y + order[i])
            for d, neighbour in enumerate((wx(x - 1), wx(x + 1))):
                p = piece(neighbour, yy)
                arrived(xg.at[p], gx.at[d, i, 0])
                send(xg.at[p, :, halves[d]], gx.at[d, i, 1], xdev[d])
                to_sibling(p)

        p = piece(x, y)
        send(xg.at[p], gy.at[0, 0, 0], yup)
        send(xg.at[p], gy.at[0, 1, 0], ydown)
        along_x(0)
        for k in range(1, HY + 1):
            for d in range(2):
                p = piece(x, wy(y - k if d == 0 else y + k))
                if k < HY:
                    arrived(xg.at[p], gy.at[0, d, k - 1])
                    sub = xg.at[p] if k < HY - 1 else xg.at[p, :, halves[d]]
                    send(sub, gy.at[0, d, k], ydev[d])
                else:
                    arrived(xg.at[p, :, halves[d]], gy.at[0, d, k - 1])
            if k < HY:
                along_x(2 * k - 1)
                along_x(2 * k)
                for i in [0] if k == 1 else [2 * k - 3, 2 * k - 2]:
                    onward_x(i)
            else:
                along_x(2 * k - 1)
                for i in (2 * k - 3, 2 * k - 2, 2 * k - 1):
                    onward_x(i)
        for i in range(NY):
            p = piece(wx(x + 2), wy(y + order[i]))
            for d in range(2):
                arrived(xg.at[p, :, halves[d]], gx.at[d, i, 1])
            to_sibling(p)

    def gather_x_then_y():
        def piece(xx, yy):
            return PER + xx * NY + yy

        def begin_y(j, xx):
            p = piece(xx, y)
            send(xg.at[p], gy.at[j, 0, 0], yup)
            send(xg.at[p], gy.at[j, 1, 0], ydown)
            to_sibling(p)

        xorder = [x, wx(x - 1), wx(x + 1), wx(x + 2)]
        p = piece(x, y)
        send(xg.at[p], gx.at[0, 0, 0], right)
        send(xg.at[p], gx.at[1, 0, 0], left)
        begin_y(0, x)
        for d in range(2):
            p = piece(xorder[1 + d], y)
            arrived(xg.at[p], gx.at[d, 0, 0])
            send(xg.at[p, :, halves[d]], gx.at[d, 0, 1], xdev[d])
            begin_y(1 + d, xorder[1 + d])
        p = piece(xorder[3], y)
        for d in range(2):
            arrived(xg.at[p, :, halves[d]], gx.at[d, 0, 1])
        begin_y(3, xorder[3])
        for k in range(1, HY + 1):
            for j in range(NX):
                for d in range(2):
                    p = piece(xorder[j], wy(y - k if d == 0 else y + k))
                    if k < HY:
                        arrived(xg.at[p], gy.at[j, d, k - 1])
                        sub = xg.at[p] if k < HY - 1 else xg.at[p, :, halves[d]]
                        send(sub, gy.at[j, d, k], ydev[d])
                        to_sibling(p)
                    else:
                        arrived(xg.at[p, :, halves[d]], gy.at[j, d, k - 1])
                        if d == 1:
                            to_sibling(p)

    pl.when(c == 0)(gather_y_then_x)
    pl.when(c == 1)(gather_x_then_y)
    arrived(xg.at[pl.ds((1 - c) * PER, PER)], d_recv)

    for load in loads:
        load.wait()

    def rows_of(a, i):
        return xg[a * PER + i * NY : a * PER + (i + 1) * NY].reshape(ROWS, SL)

    pre = dot_nn(rows_of(0, 0), wgu[0])
    d_hidden = dot_nt(rows_of(1, 0), wd[0])
    for i in range(1, NX):
        pre = pre + dot_nn(rows_of(0, i), wgu[i])
        d_hidden = d_hidden + dot_nt(rows_of(1, i), wd[i])
    gate_pre, up_pre = pre[:, :HID], pre[:, HID:]
    sigma = jax.nn.sigmoid(gate_pre)
    silu = gate_pre * sigma
    hid[...] = (silu * up_pre).astype(BF16)
    dgu[:, :HID] = (d_hidden * up_pre * sigma * (1.0 + gate_pre * (1.0 - sigma))).astype(BF16)
    dgu[:, HID:] = (d_hidden * silu).astype(BF16)

    def pieces(v):
        return v.reshape(NY, PIECE, SL)

    def partial_chunk(j, carry):
        xx = wx(x + 2 - j)
        span = pl.ds(xx * NY, NY)

        @pl.when(c == 0)
        def _():
            sib_out[span] = pieces(dot_nt(dgu[...], wgu[xx])).astype(BF16)
            remote(sib_out.at[span], sib_in.at[span], p_send.at[j], p_recv.at[j], sibling).start()
            part[span] = pieces(dot_nn(hid[...], wd[xx]))

        @pl.when(c == 1)
        def _():
            sib_out[span] = pieces(dot_nn(hid[...], wd[xx])).astype(BF16)
            remote(sib_out.at[span], sib_in.at[span], p_send.at[j], p_recv.at[j], sibling).start()
            part[span] = pieces(dot_nt(dgu[...], wgu[xx]))

        return carry

    lax.fori_loop(0, NX, partial_chunk, 0)

    def weight_grads(i, carry):
        rows_x = xg[pl.ds(i * NY, NY)].reshape(ROWS, SL)
        rows_g = xg[pl.ds(PER + i * NY, NY)].reshape(ROWS, SL)
        both = dot_tn(rows_x, dgu[...])
        ggs[i] = both[:, :HID].astype(BF16)
        gus[i] = both[:, HID:].astype(BF16)
        gds[i] = dot_tn(hid[...], rows_g).astype(BF16)
        return carry

    lax.fori_loop(0, NX, weight_grads, 0)
    stores = []
    for i in range(NX):
        rows = pl.ds(i * SL, SL)
        stores.append(pltpu.make_async_copy(ggs.at[i], gg_hbm.at[rows, :], o_sem.at[3 * i]))
        stores.append(pltpu.make_async_copy(gus.at[i], gu_hbm.at[rows, :], o_sem.at[3 * i + 1]))
        stores.append(pltpu.make_async_copy(gds.at[i], gd_hbm.at[:, rows], o_sem.at[3 * i + 2]))
    for store in stores:
        store.start()

    def from_sibling(j):
        arrived(sib_in.at[pl.ds(wx(x + 2 - j) * NY, NY)], p_recv.at[j])

    def own(p):
        return part[p] + sib_in[p].astype(F32)

    def reduce_x_then_y():
        def each_y(fn):
            def step(i, carry):
                fn(i)
                return carry

            lax.fori_loop(0, NY, step, 0)

        def push(d, m):
            remote(xs.at[d, m], xr.at[d, m], rx_s.at[d, m], rx_r.at[d, m], xdev[d]).start()

        from_sibling(0)
        far = wx(x + 2) * NY

        @each_y
        def _(i):
            v = own(far + i)
            xs[0, 0, i] = v[:, :HS].astype(BF16)
            xs[1, 0, i] = v[:, HS:].astype(BF16)

        push(0, 0)
        push(1, 0)
        from_sibling(1)
        from_sibling(3)
        to_r, to_l = wx(x + 1) * NY, wx(x - 1) * NY

        @each_y
        def _(i):
            v = own(to_r + i)
            part[to_r + i] = v
            xs[0, 1, i] = v[:, HS:].astype(BF16)

        push(0, 1)

        @each_y
        def _(i):
            v = own(to_l + i)
            part[to_l + i] = v
            xs[1, 1, i] = v[:, :HS].astype(BF16)

        push(1, 1)
        arrived(xr.at[0, 0], rx_r.at[0, 0])

        @each_y
        def _(i):
            xs[0, 2, i] = (part[to_r + i, :, 0:HS] + xr[0, 0, i].astype(F32)).astype(BF16)

        push(0, 2)
        arrived(xr.at[1, 0], rx_r.at[1, 0])

        @each_y
        def _(i):
            xs[1, 2, i] = (part[to_l + i, :, HS:SL] + xr[1, 0, i].astype(F32)).astype(BF16)

        push(1, 2)
        from_sibling(2)
        for m in (1, 2):
            for d in range(2):
                arrived(xr.at[d, m], rx_r.at[d, m])
        base = x * NY

        @each_y
        def _(i):
            v = own(base + i)
            part[base + i, :, 0:HS] = v[:, :HS] + xr[0, 2, i].astype(F32) + xr[1, 1, i].astype(F32)
            part[base + i, :, HS:SL] = v[:, HS:] + xr[0, 1, i].astype(F32) + xr[1, 2, i].astype(F32)

        for t in range(HY):
            for d in range(2):
                p = base + wy(y + HY - t if d == 0 else y - HY + t)
                y_step(0, d, t, part[p])
        arrived(yr.at[0, 0, HY - 1], ry_r.at[0, 0, HY - 1])
        arrived(yr.at[0, 1, HY - 1], ry_r.at[0, 1, HY - 1])
        res[x] = part[base + y] + yr[0, 0, HY - 1].astype(F32) + yr[0, 1, HY - 1].astype(F32)

    def y_step(j, d, t, v):
        out = ys.at[j, d, t]
        if t == 0:
            h = halves[d]
            out[:, h] = (v[:, :HS] if d == 0 else v[:, HS:]).astype(BF16)
            out, into = out.at[:, h], yr.at[j, d, t].at[:, h]
        elif t == 1:
            h = halves[d]
            arrived(yr.at[j, d, 0].at[:, h], ry_r.at[j, d, 0])
            came = yr[j, d, 0, :, h].astype(F32)
            lo, hi = v[:, :HS], v[:, HS:]
            lo, hi = (lo + came, hi) if d == 0 else (lo, hi + came)
            out[:, 0:HS] = lo.astype(BF16)
            out[:, HS:SL] = hi.astype(BF16)
            into = yr.at[j, d, t]
        else:
            arrived(yr.at[j, d, t - 1], ry_r.at[j, d, t - 1])
            out[...] = (v + yr[j, d, t - 1].astype(F32)).astype(BF16)
            into = yr.at[j, d, t]
        remote(out, into, ry_s.at[j, d, t], ry_r.at[j, d, t], ydev[d]).start()

    def reduce_y_then_x():
        def pair(j, t):
            xx = wx(x + 2 - j)
            for d in range(2):
                y_step(j, d, t, own(xx * NY + wy(y + HY - t if d == 0 else y - HY + t)))

        for t in range(HY):
            for j in range(NX):
                if t == 0:
                    from_sibling(j)
                pair(j, t)

        def total(j):
            xx = wx(x + 2 - j)
            for d in range(2):
                arrived(yr.at[j, d, HY - 1], ry_r.at[j, d, HY - 1])
            res[xx] = own(xx * NY + y) + yr[j, 0, HY - 1].astype(F32) + yr[j, 1, HY - 1].astype(F32)
            return xx

        def push(d, m, v):
            xs[d, m, 0] = v.astype(BF16)
            remote(xs.at[d, m, 0], xr.at[d, m, 0], rx_s.at[d, m], rx_r.at[d, m], xdev[d]).start()

        far = total(0)
        push(0, 0, res[far, :, 0:HS])
        push(1, 0, res[far, :, HS:SL])
        to_r = total(1)
        push(0, 1, res[to_r, :, HS:SL])
        to_l = total(3)
        push(1, 1, res[to_l, :, 0:HS])
        arrived(xr.at[0, 0, 0], rx_r.at[0, 0])
        push(0, 2, res[to_r, :, 0:HS] + xr[0, 0, 0].astype(F32))
        arrived(xr.at[1, 0, 0], rx_r.at[1, 0])
        push(1, 2, res[to_l, :, HS:SL] + xr[1, 0, 0].astype(F32))
        total(2)
        for m in (1, 2):
            for d in range(2):
                arrived(xr.at[d, m, 0], rx_r.at[d, m])
        res[x, :, 0:HS] = res[x, :, 0:HS] + xr[0, 2, 0].astype(F32) + xr[1, 1, 0].astype(F32)
        res[x, :, HS:SL] = res[x, :, HS:SL] + xr[0, 1, 0].astype(F32) + xr[1, 2, 0].astype(F32)

    pl.when(c == 0)(reduce_x_then_y)
    pl.when(c == 1)(reduce_y_then_x)

    done = res[x].astype(BF16)
    back = (dot_tn(tidy0, done[:, :HS]) + dot_tn(tidy1, done[:, HS:])).astype(BF16)
    for e in range(NZ):
        slab_out[1, e] = back[e * 16 : (e + 1) * 16]
    slab_in[1, z] = slab_out[1, z]
    exchange_z(1, zb_s, zb_r)
    chosen = dot_nn(pick[...], slab_in[1].reshape(NZ * 16, HS))
    c0 = jnp.where(c == 0, comb_ref[:, 0:1], one)
    c1 = jnp.where(c == 0, comb_ref[:, 1:2], one)
    scores = [jnp.zeros((TOKB, 1), F32), jnp.zeros((TOKB, 1), F32)]
    for h, span in enumerate((span0, span1)):
        first = chosen[2 * h * TOKB : (2 * h + 1) * TOKB]
        second = chosen[(2 * h + 1) * TOKB : (2 * h + 2) * TOKB]
        fin[tp, :, h * HS : (h + 1) * HS] = (c0 * first + c1 * second).astype(BF16)
        g = go_ref[:, span].astype(F32)
        scores[0] = scores[0] + jnp.sum(g * first, axis=1, keepdims=True)
        scores[1] = scores[1] + jnp.sum(g * second, axis=1, keepdims=True)
    lane = lax.broadcasted_iota(jnp.int32, (TOKB, 128), 1)
    fsc[tp] = jnp.where(lane == 0, scores[0], jnp.where(lane == 1, scores[1], 0.0))

    for d in range(1, NT):
        remote(fin.at[tp], fin.at[tp], f_s.at[0, d], f_r.at[0, d], peers_t[d - 1]).start()
        remote(fsc.at[tp], fsc.at[tp], f_s.at[1, d], f_r.at[1, d], peers_t[d - 1]).start()
    for d in range(1, NT):
        source = lax.rem(tp - d + NT, NT)
        arrived(fin.at[source], f_r.at[0, d])
        arrived(fsc.at[source], f_r.at[1, d])
    total_score = fsc[0]
    for i in range(NX):
        mixed_ref[:, i * SL : (i + 1) * SL] = fin[CORES * i]
        gtok_ref[:, i * SL : (i + 1) * SL] = fin[CORES * i + 1]
        if i:
            total_score = total_score + fsc[CORES * i]
    gcomb_ref[...] = total_score[:, 0:2]

    for store in stores:
        store.wait()
    for d in range(1, NZ):
        sent(slab_out.at[0, 0], za_s.at[d])
        sent(slab_out.at[1, 0], zb_s.at[d])
    for d in range(1, NT):
        sent(fin.at[tp], f_s.at[0, d])
        sent(fsc.at[tp], f_s.at[1, d])
    sent(xg.at[pl.ds(0, PER - 1)], g_send)
    sent(xg.at[pl.ds(c * PER, PER)], d_send)
    for j in range(NX):
        sent(sib_out.at[pl.ds(0, NY)], p_send.at[j])

    def y_sent(j):
        for d in range(2):
            sent(ys.at[j, d, 0].at[:, halves[d]], ry_s.at[j, d, 0])
            for t in range(1, HY):
                sent(ys.at[j, d, t], ry_s.at[j, d, t])

    @pl.when(c == 0)
    def _():
        for d in range(2):
            for m in range(3):
                sent(xs.at[d, m], rx_s.at[d, m])
        y_sent(0)

    @pl.when(c == 1)
    def _():
        for d in range(2):
            for m in range(3):
                sent(xs.at[d, m, 0], rx_s.at[d, m])
        for j in range(NX):
            y_sent(j)


def solution(mesh, cap=CAP, planes=8):
    NT = mesh.shape["tp"]
    NX, NZ = NT // CORES, planes
    NY = mesh.shape["ep"] // NZ

    def step(tokens, expert_ids, combine, grad_out, gate_weight, up_weight, down_weight):
        tokb, d = tokens.shape
        hidden = gate_weight.shape[1]
        sl, piece, per = d // NX, NZ * cap, NX * NY
        hs, rows, half_y = sl // 2, NY * piece, NY // 2
        dma, vmem, hbm = pltpu.SemaphoreType.DMA, pltpu.VMEM, pl.BlockSpec(memory_space=pl.ANY)
        held = pl.BlockSpec(memory_space=pltpu.VMEM)
        return pl.pallas_call(
            functools.partial(kernel, (NX, NY, NZ, cap)),
            out_shape=(
                jax.ShapeDtypeStruct((tokb, d), BF16),
                jax.ShapeDtypeStruct((tokb, d), BF16),
                jax.ShapeDtypeStruct(combine.shape, F32),
                jax.ShapeDtypeStruct(gate_weight.shape, BF16),
                jax.ShapeDtypeStruct(up_weight.shape, BF16),
                jax.ShapeDtypeStruct(down_weight.shape, BF16),
            ),
            in_specs=[held] * 4 + [hbm] * 3,
            out_specs=[held] * 3 + [hbm] * 3,
            scratch_shapes=[
                vmem((2 * per, piece, sl), BF16),
                vmem((per, piece, sl), F32),
                vmem((per, piece, sl), BF16),
                vmem((per, piece, sl), BF16),
                vmem((2, 3, NY, piece, hs), BF16),
                vmem((2, 3, NY, piece, hs), BF16),
                vmem((NX, 2, half_y, piece, sl), BF16),
                vmem((NX, 2, half_y, piece, sl), BF16),
                vmem((NX, piece, sl), F32),
                vmem((2, NZ, 16, hs), BF16),
                vmem((2, NZ, 16, hs), BF16),
                vmem((NT, tokb, sl), BF16),
                vmem((NT, tokb, 128), F32),
                vmem((4 * tokb, NZ * 16), BF16),
                vmem((NX, sl, 2 * hidden), BF16),
                vmem((NX, hidden, sl), BF16),
                vmem((rows, hidden), BF16),
                vmem((rows, 2 * hidden), BF16),
                vmem((NX, sl, hidden), BF16),
                vmem((NX, sl, hidden), BF16),
                vmem((NX, hidden, sl), BF16),
                dma((3 * NX,)),
                dma((NZ,)), dma((NZ,)), dma((NZ,)), dma((NZ,)),
                dma((2, NY, 2)), dma((NX, 2, half_y)),
                dma(()), dma(()), dma(()),
                dma((NX,)), dma((NX,)),
                dma((2, 3)), dma((2, 3)),
                dma((NX, 2, half_y)), dma((NX, 2, half_y)),
                dma((2, NT)), dma((2, NT)),
                dma((3 * NX,)),
            ],
            compiler_params=pltpu.CompilerParams(
                collective_id=0, has_side_effects=True, vmem_limit_bytes=56 * 2**20
            ),
        )(expert_ids, combine, tokens, grad_out, gate_weight, up_weight, down_weight)

    return jax.shard_map(
        step,
        mesh=mesh,
        in_specs=(
            P("ep", None),
            P("ep", None),
            P("ep", None),
            P("ep", None),
            P(None, ("ep", "tp")),
            P(None, ("ep", "tp")),
            P(("ep", "tp"), None),
        ),
        out_specs=(
            P("ep", None),
            P("ep", None),
            P("ep", None),
            P(None, ("ep", "tp")),
            P(None, ("ep", "tp")),
            P(("ep", "tp"), None),
        ),
        check_vma=False,
    )
```

time: 683 us -> 102 us (0.15)
  the two profiles are of different devices: /device:TPU:112 before, /device:TPU:1 now
where the time goes in v1:
time: 102 us
  Pallas kernels  91 us (89%)
  local copies, waits for them, and re-layouts  10 us (10%)
    pallas_call x1, Pallas kernels, step(): pl.pallas_call(functools.partial(kernel, (NX, NY, NZ, cap)), out_shape=(j...  91 us
    unnamed x17, local copies, waits for them, and re-layouts  9.38 us

profile of v1, /device:TPU:1, one launch (start us, length us, event | category | flops | bytes accessed | tf_op | source)
XLA Modules:
  0.0 101.7 jit_solution(6208428900200606903)
XLA Ops:
  0.6 0.0 copy-start.4
  0.6 1.4 %copy.13.ids_ref = s32[16,2]{1,0:T(8,128)} copy(s32[16,2]{0,1:T(2,128)} %param.8) | data formatting | bytes 256 | tf_op args[1]
  2.0 0.0 copy-done.4
  2.0 0.7 copy.14.comb_ref
  2.7 91.0 %shard_map.118 = (bf16[16,3072]{1,0:T(8,128)(2,1)}, bf16[16,3072]{1,0:T(8,128)(2,1)}, f32[16,2]{1,0:T(8,128)}, bf16[3072,128]{1,0:T(8,128)(2,1)}, bf16[3072,128]{1,0:T(8,128)(2,1)}, /*index=5*/bf16[128,3072]{1,0:T(8,128)(2,1)}) custom-call(s32[16,2]{1,0:T(8,128)} %copy.13.ids_ref, f32[16,2]{1,0:T(8,128)} %copy.14.comb_ref, bf16[16,3072]{1,0:T(8,128)(2,1)} %tok_ref.1, ...), custom_call_target="tpu_custom_call" | custom-call | tf_op jit(solution)/shard_map/pallas_call | solution.py:538
  93.7 0.0 copy-start.3
  93.7 0.7 copy-done.3
  94.4 0.6 copy.15
  95.0 0.0 copy-start.2
  95.0 1.6 %copy.21 = bf16[16,3072]{1,0:T(8,128)(2,1)} copy(bf16[16,3072]{1,0:T(8,128)(2,1)} %get-tuple-element.18) | data formatting | bytes 196608
  96.6 0.0 copy-done.2
  96.6 0.6 copy.22
  97.2 0.0 copy-start.1
  97.2 2.1 %copy.23 = bf16[3072,128]{1,0:T(8,128)(2,1)} copy(bf16[3072,128]{1,0:T(8,128)(2,1)} %get-tuple-element.21) | data formatting | bytes 1572864
  99.4 0.0 copy-done.1
  99.4 0.0 copy-start
  99.4 0.9 copy.24
  100.2 0.5 copy-done
  100.8 0.9 copy.25
Async XLA Ops:
  0.6 1.4 %copy-start.4 = (f32[16,2]{0,1:T(2,128)S(1)}, f32[16,2]{0,1:T(2,128)}, u32[]{:S(2)}) copy-start(f32[16,2]{0,1:T(2,128)} %param.9) | copy-start | bytes 388
  93.7 0.7 copy-start.3
  95.0 1.6 %copy-start.2 = (bf16[16,3072]{1,0:T(8,128)(2,1)S(1)}, bf16[16,3072]{1,0:T(8,128)(2,1)}, u32[]{:S(2)}) copy-start(bf16[16,3072]{1,0:T(8,128)(2,1)} %get-tuple-element.19) | copy-start | bytes 294916
  97.2 2.1 %copy-start.1 = (bf16[3072,128]{1,0:T(8,128)(2,1)S(1)}, bf16[3072,128]{1,0:T(8,128)(2,1)}, u32[]{:S(2)}) copy-start(bf16[3072,128]{1,0:T(8,128)(2,1)} %get-tuple-element.22) | copy-start | bytes 2359300
  99.4 1.4 %copy-start = (bf16[128,3072]{1,0:T(8,128)(2,1)S(1)}, bf16[128,3072]{1,0:T(8,128)(2,1)}, u32[]{:S(2)}) copy-start(bf16[128,3072]{1,0:T(8,128)(2,1)} %get-tuple-element.23) | copy-start | bytes 2359300

commit v2 on v1

v2 whole, which is shorter than its diff:
```python
import functools

import jax
import jax.numpy as jnp
from jax import lax
from jax.experimental import pallas as pl
from jax.experimental.pallas import tpu as pltpu
from jax.sharding import PartitionSpec as P

CAP = 6
CORES = 2
MESH = pl.DeviceIdType.MESH
F32 = jnp.float32
BF16 = jnp.bfloat16


def dot_nn(a, b):
    return jnp.dot(a, b, preferred_element_type=F32)


def dot_nt(a, b):
    return lax.dot_general(a, b, (((1,), (1,)), ((), ())), preferred_element_type=F32)


def dot_tn(a, b):
    return lax.dot_general(a, b, (((0,), (0,)), ((), ())), preferred_element_type=F32)


def kernel(
    dims,
    ids_ref, comb_ref, tok_hbm, go_hbm, gate_hbm, up_hbm, down_hbm,
    mixed_ref, gtok_ref, gcomb_ref, gg_ref, gu_ref, gd_ref,
    xg, part, xs, xr, ys, yr, res,
    slab_out, slab_in, fin, fsc, pick, src, gos, wgu, wd, hid, dgu,
    w_sem, t_sem, za_s, za_r, zb_s, zb_r, gx, gy, g_send, d_send, d_recv,
    p_send, p_recv, rx_s, rx_r, ry_s, ry_r, f_s, f_r,
):
    NX, NY, NZ, CAPA = dims
    PIECE = NZ * CAPA
    TOKB, D = tok_hbm.shape
    SL = D // NX
    HS = SL // 2
    ROWS = NY * PIECE
    PER = NX * NY
    HID = wd.shape[1] // 2

    ep, tp = lax.axis_index("ep"), lax.axis_index("tp")
    c, x = lax.rem(tp, CORES), lax.div(tp, CORES)
    y, z = lax.rem(ep, NY), lax.div(ep, NY)

    def wx(v):
        return lax.rem(v + 2 * NX, NX)

    def wy(v):
        return lax.rem(v + 2 * NY, NY)

    def at(xx, yy, zz, cc):
        return (zz * NY + yy, xx * CORES + cc)

    yup, ydown = at(x, wy(y + 1), z, c), at(x, wy(y - 1), z, c)
    sibling = at(x, y, z, 1 - c)

    def remote(src, dst, ssem, rsem, device):
        return pltpu.make_async_remote_copy(
            src_ref=src, dst_ref=dst, send_sem=ssem, recv_sem=rsem,
            device_id=device, device_id_type=MESH,
        )

    def arrived(dst, rsem):
        remote(dst, dst, rsem, rsem, sibling).wait_recv()

    def sent(src, ssem):
        remote(src, src, ssem, ssem, sibling).wait_send()

    barrier = pltpu.get_barrier_semaphore()
    peers_z = [at(x, y, lax.rem(z + d, NZ), c) for d in range(1, NZ)]
    NT = NX * CORES
    peers_t = [(ep, lax.rem(tp + d, NT)) for d in range(1, NT)]
    far_up, far_down = at(x, wy(y + 2), z, c), at(x, wy(y - 2), z, c)
    partners = peers_z + peers_t + [yup, ydown, far_up, far_down]
    ynear, yfar = (yup, ydown), (far_up, far_down)
    xdev = [at(wx(x + k), y, z, c) for k in (2, 1, NX - 1)]
    for device in partners:
        pl.semaphore_signal(barrier, inc=1, device_id=device, device_id_type=MESH)

    features = pl.ds(pl.multiple_of(x * SL, 128), SL)

    @pl.when(c == 0)
    def _():
        pltpu.make_async_copy(tok_hbm.at[:, features], src, t_sem.at[0]).start()

    @pl.when(c == 1)
    def _():
        pltpu.make_async_copy(go_hbm.at[:, features], src, t_sem.at[0]).start()

    load_go = pltpu.make_async_copy(go_hbm.at[:, features], gos, t_sem.at[1])
    load_go.start()
    own_units, sib_units = (pl.ds(0, HID), pl.ds(HID, HID))
    own_pair, sib_pair = (pl.ds(0, 2 * HID), pl.ds(2 * HID, 2 * HID))
    loads = []
    for i in range(NX):
        rows = pl.ds(i * SL, SL)
        loads.append(pltpu.make_async_copy(gate_hbm.at[rows, :], wgu.at[i, :, pl.ds(0, HID)], w_sem.at[3 * i]))
        loads.append(pltpu.make_async_copy(up_hbm.at[rows, :], wgu.at[i, :, pl.ds(HID, HID)], w_sem.at[3 * i + 1]))
        loads.append(pltpu.make_async_copy(down_hbm.at[:, rows], wd.at[i, own_units], w_sem.at[3 * i + 2]))
    for load in loads:
        load.start()

    lane = lax.broadcasted_iota(jnp.int32, (TOKB, NZ * 16), 1)
    expert, place = lax.shift_right_logical(lane, 4), lane & 15
    diagonal = lax.broadcasted_iota(jnp.int32, (TOKB, TOKB), 0) == lax.broadcasted_iota(jnp.int32, (TOKB, TOKB), 1)

    def column(ref, k):
        return jnp.sum(jnp.where(diagonal, ref[k : k + 1, :].astype(F32), 0.0), axis=1, keepdims=True)

    id0, id1 = column(ids_ref, 0).astype(jnp.int32), column(ids_ref, 1).astype(jnp.int32)
    cw0, cw1 = column(comb_ref, 0), column(comb_ref, 1)
    is0, is1 = id0 == expert, id1 == expert
    named = jnp.where(is0 | is1, 1.0, 0.0)
    earlier = jnp.where(
        lax.broadcasted_iota(jnp.int32, (TOKB, TOKB), 0) > lax.broadcasted_iota(jnp.int32, (TOKB, TOKB), 1), 1.0, 0.0
    )
    rank = dot_nn(earlier.astype(BF16), named.astype(BF16)).astype(jnp.int32)
    hit0 = rank == place
    hit1 = (rank + CAPA == place) & (rank < CAPA)
    hit0 = hit0 & (place < CAPA)
    for g, mask in enumerate((is0 & hit0, is1 & hit0, is0 & hit1, is1 & hit1)):
        pick[g * TOKB : (g + 1) * TOKB, :] = jnp.where(mask, 1.0, 0.0).astype(BF16)

    one = jnp.ones((TOKB, 1), F32)
    w0 = jnp.where(c == 0, one, cw0)
    w1 = jnp.where(c == 0, one, cw1)
    spans = (slice(0, HS), slice(HS, SL))
    pltpu.make_async_copy(gos, src, t_sem.at[0]).wait()
    sources = []
    for span in spans:
        v = src[:, span].astype(F32)
        sources += [(v * w0).astype(BF16), (v * w1).astype(BF16)]
    slabs = dot_tn(pick[...], jnp.concatenate(sources, axis=0)).astype(BF16)
    for e in range(NZ):
        slab_out[0, e] = slabs[e * 16 : (e + 1) * 16]
    slab_in[0, z] = slab_out[0, z]

    pl.semaphore_wait(barrier, len(partners))

    def give_weights():
        for load in loads:
            load.wait()

        @pl.when(c == 0)
        def _():
            remote(wgu.at[:, :, own_pair], wgu.at[:, :, sib_pair], p_send.at[0], p_recv.at[0], sibling).start()

        @pl.when(c == 1)
        def _():
            remote(wd.at[:, own_units], wd.at[:, sib_units], p_send.at[0], p_recv.at[0], sibling).start()

    def exchange_z(which, s_sem, r_sem):
        for d in range(1, NZ):
            remote(
                slab_out.at[which, lax.rem(z + d, NZ)], slab_in.at[which, z],
                s_sem.at[d], r_sem.at[d], peers_z[d - 1],
            ).start()
        if which == 0:
            give_weights()
        for d in range(1, NZ):
            arrived(slab_in.at[which, lax.rem(z - d + NZ, NZ)], r_sem.at[d])

    exchange_z(0, za_s, za_r)

    row = lax.broadcasted_iota(jnp.int32, (PIECE, NZ * 16), 0)
    col = lax.broadcasted_iota(jnp.int32, (PIECE, NZ * 16), 1)
    block, inner = lax.shift_right_logical(col, 4), col & 15
    tidy0 = jnp.where((block * CAPA + inner == row) & (inner < CAPA), 1.0, 0.0).astype(BF16)
    tidy1 = jnp.where(
        (block * CAPA + inner - CAPA == row) & (inner >= CAPA) & (inner < 2 * CAPA), 1.0, 0.0
    ).astype(BF16)
    got = slab_in[0].reshape(NZ * 16, HS)
    mine = c * PER + x * NY + y
    xg[mine, :, 0:HS] = dot_nn(tidy0, got).astype(BF16)
    xg[mine, :, HS:SL] = dot_nn(tidy1, got).astype(BF16)

    halves = (pl.ds(0, HS), pl.ds(HS, HS))
    HY = NY // 2
    order = (0, -1, 1, -2, 2, -3, 3, HY)

    def to_sibling(p):
        remote(xg.at[p], xg.at[p], d_send, d_recv, sibling).start()

    def send(ref, sem, device):
        remote(ref, ref, g_send, sem, device).start()

    def along_x(p, i):
        for k in range(NX - 1):
            send(xg.at[p], gx.at[k, i], xdev[k])

    def from_x(k):
        return wx(x - (2, 1, -1)[k])

    def begin_y(j, p, short):
        for d in range(2):
            if short:
                send(xg.at[p], gy.at[j, d, 1], yfar[d])
            send(xg.at[p], gy.at[j, d, 0], ynear[d])

    def onward_y(j, d, s, piece_at, short):
        p = piece_at(wy(y - s - 1 if d == 0 else y + s + 1))
        if s == HY - 1:
            arrived(xg.at[p, :, halves[d]], gy.at[j, d, s])
            return p
        arrived(xg.at[p], gy.at[j, d, s])
        if s == 0 and not short:
            send(xg.at[p], gy.at[j, d, 1], ynear[d])
        if s == 1:
            send(xg.at[p], gy.at[j, d, 2], ynear[d])
            send(xg.at[p, :, halves[d]], gy.at[j, d, 3], yfar[d])
        return p

    def gather_y_then_x():
        def piece_at(yy):
            return x * NY + yy

        p = piece_at(y)
        begin_y(0, p, True)
        along_x(p, 0)
        to_sibling(p)
        for s in range(HY):
            for d in range(2):
                p = onward_y(0, d, s, piece_at, True)
                if s < HY - 1 or d == 1:
                    along_x(p, 2 * s + 1 if s == HY - 1 else 2 * s + 1 + d)
                    to_sibling(p)
        for i in range(NY):
            for k in range(NX - 1):
                p = from_x(k) * NY + wy(y + order[i])
                arrived(xg.at[p], gx.at[k, i])
                to_sibling(p)

    def gather_x_then_y():
        def piece_of(xx):
            return lambda yy: PER + xx * NY + yy

        p = piece_of(x)(y)
        along_x(p, 0)
        begin_y(0, p, False)
        to_sibling(p)
        streams = [(0, piece_of(x))] + [(1 + k, piece_of(from_x(k))) for k in (1, 2, 0)]
        for j, piece_at in streams[1:]:
            p = piece_at(y)
            arrived(xg.at[p], gx.at[j - 1, 0])
            begin_y(j, p, False)
            to_sibling(p)
        for s in range(HY):
            for j, piece_at in streams:
                for d in range(2):
                    p = onward_y(j, d, s, piece_at, False)
                    if s < HY - 1 or d == 1:
                        to_sibling(p)

    pl.when(c == 0)(gather_y_then_x)
    pl.when(c == 1)(gather_x_then_y)
    arrived(xg.at[pl.ds((1 - c) * PER, PER)], d_recv)

    def rows_of(a, i):
        return xg[a * PER + i * NY : a * PER + (i + 1) * NY].reshape(ROWS, SL)

    pre = dot_nn(rows_of(0, 0), wgu[0, :, own_pair])
    d_hidden = dot_nt(rows_of(1, 0), wd[0, own_units])
    for i in range(1, NX):
        pre = pre + dot_nn(rows_of(0, i), wgu[i, :, own_pair])
        d_hidden = d_hidden + dot_nt(rows_of(1, i), wd[i, own_units])
    gate_pre, up_pre = pre[:, :HID], pre[:, HID:]
    sigma = jax.nn.sigmoid(gate_pre)
    silu = gate_pre * sigma
    hid[:, own_units] = (silu * up_pre).astype(BF16)
    dgu[:, pl.ds(0, HID)] = (d_hidden * up_pre * sigma * (1.0 + gate_pre * (1.0 - sigma))).astype(BF16)
    dgu[:, pl.ds(HID, HID)] = (d_hidden * silu).astype(BF16)

    @pl.when(c == 0)
    def _():
        remote(dgu.at[:, own_pair], dgu.at[:, sib_pair], p_send.at[1], p_recv.at[1], sibling).start()

    @pl.when(c == 1)
    def _():
        remote(hid.at[:, own_units], hid.at[:, sib_units], p_send.at[1], p_recv.at[1], sibling).start()

    def weight_grads(first, last):
        def step(i, carry):
            rows_x = xg[pl.ds(i * NY, NY)].reshape(ROWS, SL)
            rows_g = xg[pl.ds(PER + i * NY, NY)].reshape(ROWS, SL)
            both = dot_tn(rows_x, dgu[:, own_pair])
            span = pl.ds(pl.multiple_of(i * SL, 128), SL)
            gg_ref[span, :] = both[:, :HID].astype(BF16)
            gu_ref[span, :] = both[:, HID:].astype(BF16)
            gd_ref[:, span] = dot_tn(hid[:, own_units], rows_g).astype(BF16)
            return carry

        lax.fori_loop(first, last, step, 0)

    weight_grads(0, NX // 2)

    def partial_chunk(j, carry):
        xx = wx(x + 2 - j)
        span = pl.ds(xx * NY, NY)

        @pl.when(c == 0)
        def _():
            part[span] = dot_nn(hid[...], wd[xx]).reshape(NY, PIECE, SL)

        @pl.when(c == 1)
        def _():
            part[span] = dot_nt(dgu[...], wgu[xx]).reshape(NY, PIECE, SL)

        return carry

    @pl.when(c == 0)
    def _():
        arrived(wd.at[:, sib_units], p_recv.at[0])
        arrived(hid.at[:, sib_units], p_recv.at[1])

    @pl.when(c == 1)
    def _():
        arrived(wgu.at[:, :, sib_pair], p_recv.at[0])
        arrived(dgu.at[:, sib_pair], p_recv.at[1])

    lax.fori_loop(0, NX, partial_chunk, 0)

    def own(p):
        return part[p]

    def y_out(j, d, s, v):
        out, into = ys.at[j, d, s], yr.at[j, d, s]
        if s == HY - 1:
            out, into = out.at[:, halves[d]], into.at[:, halves[d]]
            v = v[:, :HS] if d == 0 else v[:, HS:]
        out[...] = v.astype(BF16)
        hop = yfar if s == HY - 1 or (s == 1 and c_short[0]) else ynear
        remote(out, into, ry_s.at[j, d, s], ry_r.at[j, d, s], hop[d]).start()

    def y_came(j, d, s):
        into = yr.at[j, d, s]
        if s == HY - 1:
            into = into.at[:, halves[d]]
        arrived(into, ry_r.at[j, d, s])
        return into[...].astype(F32)

    def y_first(j, get):
        for d in range(2):
            y_out(j, d, 2, get(3 - 6 * d))
        v = get(HY)
        for d in range(2):
            y_out(j, d, 3, v)

    def y_second(j, d, get):
        v = get(2 - 4 * d) + y_came(j, d, 2)
        half = y_came(j, d, 3)
        lo, hi = v[:, :HS], v[:, HS:]
        lo, hi = (lo + half, hi) if d == 0 else (lo, hi + half)
        y_out(j, d, 1, jnp.concatenate([lo, hi], axis=1))

    def x_out(k, i, v):
        xs[k, i] = v.astype(BF16)
        remote(xs.at[k, i], xr.at[k, i], rx_s.at[k, i], rx_r.at[k, i], xdev[k]).start()

    def x_came(i):
        v = None
        for k in range(NX - 1):
            arrived(xr.at[k, i], rx_r.at[k, i])
            w = xr[k, i].astype(F32)
            v = w if v is None else v + w
        return v

    c_short = [False]
    back_order = (3, -3, HY, 2, -2, 1, -1, 0)
    chunk_of = (0, 1, 3)

    def at_y(off):
        return wy(y + off)

    def begin_x_then_y():
        for i, off in enumerate(back_order):
            for k in range(NX - 1):
                x_out(k, i, own(wx(x + 2 - chunk_of[k]) * NY + at_y(off)))

    def begin_y_then_x():
        for j in range(NX):
            y_first(j, lambda off: own(wx(x + 2 - j) * NY + at_y(off)))

    pl.when(c == 0)(begin_x_then_y)
    pl.when(c == 1)(begin_y_then_x)

    weight_grads(NX // 2, NX)

    def end_x_then_y():
        c_short[0] = True

        def get(off):
            return own(x * NY + at_y(off)) + x_came(back_order.index(off))

        y_first(0, get)
        for d in range(2):
            y_second(0, d, get)
        for d in range(2):
            y_out(0, d, 0, get(1 - 2 * d))
        v = get(0)
        for s in range(2):
            for d in range(2):
                v = v + y_came(0, d, s)
        res[x] = v

    def end_y_then_x():
        c_short[0] = False

        def get(j):
            return lambda off: own(wx(x + 2 - j) * NY + at_y(off))

        for j in range(NX):
            for d in range(2):
                y_second(j, d, get(j))
        for j in range(NX):
            for d in range(2):
                y_out(j, d, 0, get(j)(1 - 2 * d) + y_came(j, d, 1))
        for j in range(NX):
            v = get(j)(0) + y_came(j, 0, 0) + y_came(j, 1, 0)
            if j in chunk_of:
                x_out(chunk_of.index(j), 0, v)
            else:
                res[x] = v
        res[x] = res[x] + x_came(0)

    pl.when(c == 0)(end_x_then_y)
    pl.when(c == 1)(end_y_then_x)

    done = res[x].astype(BF16)
    back = (dot_tn(tidy0, done[:, :HS]) + dot_tn(tidy1, done[:, HS:])).astype(BF16)
    for e in range(NZ):
        slab_out[1, e] = back[e * 16 : (e + 1) * 16]
    slab_in[1, z] = slab_out[1, z]
    exchange_z(1, zb_s, zb_r)
    chosen = dot_nn(pick[...], slab_in[1].reshape(NZ * 16, HS))
    c0 = jnp.where(c == 0, cw0, one)
    c1 = jnp.where(c == 0, cw1, one)
    scores = [jnp.zeros((TOKB, 1), F32), jnp.zeros((TOKB, 1), F32)]
    load_go.wait()
    for h, span in enumerate(spans):
        first = chosen[2 * h * TOKB : (2 * h + 1) * TOKB]
        second = chosen[(2 * h + 1) * TOKB : (2 * h + 2) * TOKB]
        fin[tp, :, h * HS : (h + 1) * HS] = (c0 * first + c1 * second).astype(BF16)
        g = gos[:, span].astype(F32)
        scores[0] = scores[0] + jnp.sum(g * first, axis=1, keepdims=True)
        scores[1] = scores[1] + jnp.sum(g * second, axis=1, keepdims=True)
    lane = lax.broadcasted_iota(jnp.int32, (TOKB, 128), 1)
    fsc[tp] = jnp.where(lane == 0, scores[0], jnp.where(lane == 1, scores[1], 0.0))

    for d in range(1, NT):
        remote(fin.at[tp], fin.at[tp], f_s.at[0, d], f_r.at[0, d], peers_t[d - 1]).start()
        remote(fsc.at[tp], fsc.at[tp], f_s.at[1, d], f_r.at[1, d], peers_t[d - 1]).start()
    for d in range(1, NT):
        source = lax.rem(tp - d + NT, NT)
        arrived(fin.at[source], f_r.at[0, d])
        arrived(fsc.at[source], f_r.at[1, d])
    total_score = fsc[0]
    for i in range(NX):
        mixed_ref[:, i * SL : (i + 1) * SL] = fin[CORES * i]
        gtok_ref[:, i * SL : (i + 1) * SL] = fin[CORES * i + 1]
        if i:
            total_score = total_score + fsc[CORES * i]
    for k in range(2):
        gcomb_ref[k : k + 1, :] = jnp.sum(jnp.where(diagonal, total_score[:, k : k + 1], 0.0), axis=0, keepdims=True)

    for d in range(1, NZ):
        sent(slab_out.at[0, 0], za_s.at[d])
        sent(slab_out.at[1, 0], zb_s.at[d])
    for d in range(1, NT):
        sent(fin.at[tp], f_s.at[0, d])
        sent(fsc.at[tp], f_s.at[1, d])
    sent(xg.at[pl.ds(0, PER - 1)], g_send)
    sent(xg.at[pl.ds(c * PER, PER)], d_send)

    def y_sent(j):
        for d in range(2):
            sent(ys.at[j, d, HY - 1].at[:, halves[d]], ry_s.at[j, d, HY - 1])
            for t in range(HY - 1):
                sent(ys.at[j, d, t], ry_s.at[j, d, t])

    @pl.when(c == 0)
    def _():
        sent(wgu.at[:, :, own_pair], p_send.at[0])
        sent(dgu.at[:, own_pair], p_send.at[1])
        for k in range(NX - 1):
            for i in range(NY):
                sent(xs.at[k, i], rx_s.at[k, i])
        y_sent(0)

    @pl.when(c == 1)
    def _():
        sent(wd.at[:, own_units], p_send.at[0])
        sent(hid.at[:, own_units], p_send.at[1])
        for k in range(NX - 1):
            sent(xs.at[k, 0], rx_s.at[k, 0])
        for j in range(NX):
            y_sent(j)


def solution(mesh, cap=CAP, planes=8):
    NT = mesh.shape["tp"]
    NX, NZ = NT // CORES, planes
    NY = mesh.shape["ep"] // NZ

    def step(tokens, expert_ids, combine, grad_out, gate_weight, up_weight, down_weight):
        tokb, d = tokens.shape
        hidden = gate_weight.shape[1]
        sl, piece, per = d // NX, NZ * cap, NX * NY
        hs, rows, half_y = sl // 2, NY * piece, NY // 2
        dma, vmem, hbm = pltpu.SemaphoreType.DMA, pltpu.VMEM, pl.BlockSpec(memory_space=pl.ANY)
        held = pl.BlockSpec(memory_space=pltpu.VMEM)
        mixed, gtok, gcomb, gg, gu, gd = pl.pallas_call(
            functools.partial(kernel, (NX, NY, NZ, cap)),
            out_shape=(
                vmem((tokb, d), BF16),
                vmem((tokb, d), BF16),
                vmem(combine.shape[::-1], F32),
                vmem(gate_weight.shape, BF16),
                vmem(up_weight.shape, BF16),
                vmem(down_weight.shape, BF16),
            ),
            in_specs=[held] * 2 + [hbm] * 5,
            out_specs=[held] * 6,
            scratch_shapes=[
                vmem((2 * per, piece, sl), BF16),
                vmem((per, piece, sl), F32),
                vmem((NX - 1, NY, piece, sl), BF16),
                vmem((NX - 1, NY, piece, sl), BF16),
                vmem((NX, 2, half_y, piece, sl), BF16),
                vmem((NX, 2, half_y, piece, sl), BF16),
                vmem((NX, piece, sl), F32),
                vmem((2, NZ, 16, hs), BF16),
                vmem((2, NZ, 16, hs), BF16),
                vmem((NT, tokb, sl), BF16),
                vmem((NT, tokb, 128), F32),
                vmem((4 * tokb, NZ * 16), BF16),
                vmem((tokb, sl), BF16), vmem((tokb, sl), BF16),
                vmem((NX, sl, 4 * hidden), BF16),
                vmem((NX, 2 * hidden, sl), BF16),
                vmem((rows, 2 * hidden), BF16),
                vmem((rows, 4 * hidden), BF16),
                dma((3 * NX,)), dma((2,)),
                dma((NZ,)), dma((NZ,)), dma((NZ,)), dma((NZ,)),
                dma((NX - 1, NY)), dma((NX, 2, half_y)),
                dma(()), dma(()), dma(()),
                dma((2,)), dma((2,)),
                dma((NX - 1, NY)), dma((NX - 1, NY)),
                dma((NX, 2, half_y)), dma((NX, 2, half_y)),
                dma((2, NT)), dma((2, NT)),
            ],
            compiler_params=pltpu.CompilerParams(
                collective_id=0, has_side_effects=True, vmem_limit_bytes=56 * 2**20
            ),
        )(expert_ids.T, combine.T, tokens, grad_out, gate_weight, up_weight, down_weight)
        return mixed, gtok, gcomb.T, gg, gu, gd

    return jax.shard_map(
        step,
        mesh=mesh,
        in_specs=(
            P("ep", None),
            P("ep", None),
            P("ep", None),
            P("ep", None),
            P(None, ("ep", "tp")),
            P(None, ("ep", "tp")),
            P(("ep", "tp"), None),
        ),
        out_specs=(
            P("ep", None),
            P("ep", None),
            P("ep", None),
            P(None, ("ep", "tp")),
            P(None, ("ep", "tp")),
            P(("ep", "tp"), None),
        ),
        check_vma=False,
    )
```

time: 102 us -> 85.2 us (0.84)
  Pallas kernels: 91 us -> 79.9 us
  local copies, waits for them, and re-layouts: 10 us -> 4.48 us
    pallas_call x1, Pallas kernels: 91 us -> 79.9 us  [step(): pl.pallas_call(functools.partial(kernel, (NX, NY, NZ, cap)), out_shape=(v...]
    unnamed x17 -> x6, local copies, waits for them, and re-layouts: 9.38 us -> 4.48 us
where the time goes in v2:
time: 85.2 us; the launch traced here: 85 us
  Pallas kernels  79.9 us (94%)
  local copies, waits for them, and re-layouts  4.48 us (5%)
    pallas_call x1, Pallas kernels, step(): pl.pallas_call(functools.partial(kernel, (NX, NY, NZ, cap)), out_shape=(v...  79.9 us
    unnamed x6, local copies, waits for them, and re-layouts  4.48 us

profile of v2, /device:TPU:1, one launch (start us, length us, event | category | flops | bytes accessed | tf_op | source)
XLA Modules:
  0.0 85.0 jit_solution(9589125687768880630)
XLA Ops:
  0.6 79.9 %shard_map.118 = (bf16[16,3072]{1,0:T(8,128)(2,1)S(1)}, bf16[16,3072]{1,0:T(8,128)(2,1)S(1)}, f32[2,16]{1,0:T(2,128)S(1)}, bf16[3072,128]{1,0:T(8,128)(2,1)S(1)}...) custom-call(s32[2,16]{1,0:T(2,128)} %bitcast.4, f32[2,16]{1,0:T(2,128)} %bitcast.5, ...), custom_call_target="tpu_custom_call" | custom-call | tf_op jit(solution)/shard_map/pallas_call | solution.py:517
  80.5 0.6 copy.19
  81.2 0.6 copy.21
  81.7 0.6 copy.20
  82.4 0.9 %copy.22 = bf16[3072,128]{1,0:T(8,128)(2,1)} copy(bf16[3072,128]{1,0:T(8,128)(2,1)S(1)} %get-tuple-element.21) | data formatting | bytes 1572864
  83.3 0.9 %copy.23 = bf16[3072,128]{1,0:T(8,128)(2,1)} copy(bf16[3072,128]{1,0:T(8,128)(2,1)S(1)} %get-tuple-element.22) | data formatting | bytes 1572864
  84.1 0.9 %copy.24 = bf16[128,3072]{1,0:T(8,128)(2,1)} copy(bf16[128,3072]{1,0:T(8,128)(2,1)S(1)} %get-tuple-element.23) | data formatting | bytes 1572864

commit v3 on v2

--- a/solution.py
+++ b/solution.py
@@ -299,31 +299,13 @@
 
     weight_grads(0, NX // 2)
 
-    def partial_chunk(j, carry):
+    def expert_out_chunk(j):
         xx = wx(x + 2 - j)
-        span = pl.ds(xx * NY, NY)
-
-        @pl.when(c == 0)
-        def _():
-            part[span] = dot_nn(hid[...], wd[xx]).reshape(NY, PIECE, SL)
-
-        @pl.when(c == 1)
-        def _():
-            part[span] = dot_nt(dgu[...], wgu[xx]).reshape(NY, PIECE, SL)
-
-        return carry
-
-    @pl.when(c == 0)
-    def _():
-        arrived(wd.at[:, sib_units], p_recv.at[0])
-        arrived(hid.at[:, sib_units], p_recv.at[1])
-
-    @pl.when(c == 1)
-    def _():
-        arrived(wgu.at[:, :, sib_pair], p_recv.at[0])
-        arrived(dgu.at[:, sib_pair], p_recv.at[1])
-
-    lax.fori_loop(0, NX, partial_chunk, 0)
+        part[pl.ds(xx * NY, NY)] = dot_nn(hid[...], wd[xx]).reshape(NY, PIECE, SL)
+
+    def input_grad_chunk(j):
+        xx = wx(x + 2 - j)
+        part[pl.ds(xx * NY, NY)] = dot_nt(dgu[...], wgu[xx]).reshape(NY, PIECE, SL)
 
     def own(p):
         return part[p]
@@ -378,12 +360,20 @@
         return wy(y + off)
 
     def begin_x_then_y():
+        arrived(wd.at[:, sib_units], p_recv.at[0])
+        arrived(hid.at[:, sib_units], p_recv.at[1])
+        for j in chunk_of:
+            expert_out_chunk(j)
         for i, off in enumerate(back_order):
             for k in range(NX - 1):
                 x_out(k, i, own(wx(x + 2 - chunk_of[k]) * NY + at_y(off)))
+        expert_out_chunk(2)
 
     def begin_y_then_x():
+        arrived(wgu.at[:, :, sib_pair], p_recv.at[0])
+        arrived(dgu.at[:, sib_pair], p_recv.at[1])
         for j in range(NX):
+            input_grad_chunk(j)
             y_first(j, lambda off: own(wx(x + 2 - j) * NY + at_y(off)))
 
     pl.when(c == 0)(begin_x_then_y)
@@ -500,6 +490,16 @@
             sent(xs.at[k, 0], rx_s.at[k, 0])
         for j in range(NX):
             y_sent(j)
+
+
+def flush(*refs):
+    n = len(refs) // 2
+    sems = refs[-1]
+    copies = [pltpu.make_async_copy(refs[i], refs[n + i], sems.at[i]) for i in range(n)]
+    for copy in copies:
+        copy.start()
+    for copy in copies:
+        copy.wait()
 
 
 def solution(mesh, cap=CAP, planes=8):
@@ -557,6 +557,14 @@
                 collective_id=0, has_side_effects=True, vmem_limit_bytes=56 * 2**20
             ),
         )(expert_ids.T, combine.T, tokens, grad_out, gate_weight, up_weight, down_weight)
+        made = (gg, gu, gd, mixed, gtok, gcomb)
+        gg, gu, gd, mixed, gtok, gcomb = pl.pallas_call(
+            flush,
+            out_shape=tuple(jax.ShapeDtypeStruct(m.shape, m.dtype) for m in made),
+            in_specs=[held] * len(made),
+            out_specs=[hbm] * len(made),
+            scratch_shapes=[dma((len(made),))],
+        )(*[pltpu.with_memory_space_constraint(m, pltpu.VMEM) for m in made])
         return mixed, gtok, gcomb.T, gg, gu, gd
 
     return jax.shard_map(

time: 85.2 us -> 80.6 us (0.946)
  local copies, waits for them, and re-layouts: 4.48 us -> 0 us
    unnamed x6 -> x0, local copies, waits for them, and re-layouts: 4.48 us -> none
    pallas_call x1, Pallas kernels: 79.9 us -> 78.3 us  [step(): pl.pallas_call(functools.partial(kernel, (NX, NY, NZ, cap)), out_shape=(v...]
    pallas_call x0 -> x1, Pallas kernels: none -> 1.51 us  [step(): pl.pallas_call(flush, out_shape=tuple((jax.ShapeDtypeStruct(m.shape, m.dt...]
where the time goes in v3:
time: 80.6 us; the launch traced here: 80.5 us
  Pallas kernels  79.8 us (99%)
    pallas_call x1, Pallas kernels, step(): pl.pallas_call(functools.partial(kernel, (NX, NY, NZ, cap)), out_shape=(v...  78.3 us

profile of v3, /device:TPU:1, one launch (start us, length us, event | category | flops | bytes accessed | tf_op | source)
XLA Modules:
  0.0 80.5 jit_solution(5233267434763207513)
XLA Ops:
  0.6 78.3 %shard_map.118 = (bf16[16,3072]{1,0:T(8,128)(2,1)S(1)}, bf16[16,3072]{1,0:T(8,128)(2,1)S(1)}, f32[2,16]{1,0:T(2,128)S(1)}, bf16[3072,128]{1,0:T(8,128)(2,1)S(1)}...) custom-call(s32[2,16]{1,0:T(2,128)} %bitcast.3, f32[2,16]{1,0:T(2,128)} %bitcast.4, ...), custom_call_target="tpu_custom_call" | custom-call | tf_op jit(solution)/shard_map/pallas_call | solution.py:517
  79.0 1.5 %shard_map.119 = (bf16[3072,128]{1,0:T(8,128)(2,1)}, bf16[3072,128]{1,0:T(8,128)(2,1)}, bf16[128,3072]{1,0:T(8,128)(2,1)}, bf16[16,3072]{1,0:T(8,128)(2,1)}, bf16[16,3072]{1,0:T(8,128)(2,1)}, /*index=5*/f32[2,16]{1,0:T(2,128)}) custom-call(bf16[3072,128]{1,0:T(8,128)(2,1)S(1)} %get-tuple-element.18.refs_0_, bf16[3072,128]{1,0:T(8,128)(2,1)S(1)} %get-tuple-element.19.refs_1_, ...), custom_call_target="tpu_custom_call" | custom-call | tf_op jit(solution)/shard_map/pallas_call | solution.py:561

commit v4 on v3

--- a/solution.py
+++ b/solution.py
@@ -31,7 +31,7 @@
     ids_ref, comb_ref, tok_hbm, go_hbm, gate_hbm, up_hbm, down_hbm,
     mixed_ref, gtok_ref, gcomb_ref, gg_ref, gu_ref, gd_ref,
     xg, part, xs, xr, ys, yr, res,
-    slab_out, slab_in, fin, fsc, pick, src, gos, wgu, wd, hid, dgu,
+    slab_out, slab_in, fin, fsc, pick, src, gos, wgu, wd, hid, dgu, pre_ref, dh_ref,
     w_sem, t_sem, za_s, za_r, zb_s, zb_r, gx, gy, g_send, d_send, d_recv,
     p_send, p_recv, rx_s, rx_r, ry_s, ry_r, f_s, f_r,
 ):
@@ -87,11 +87,11 @@
 
     @pl.when(c == 0)
     def _():
-        pltpu.make_async_copy(tok_hbm.at[:, features], src, t_sem.at[0]).start()
+        pltpu.make_async_copy(tok_hbm, src, t_sem.at[0]).start()
 
     @pl.when(c == 1)
     def _():
-        pltpu.make_async_copy(go_hbm.at[:, features], src, t_sem.at[0]).start()
+        pltpu.make_async_copy(go_hbm, src, t_sem.at[0]).start()
 
     load_go = pltpu.make_async_copy(go_hbm.at[:, features], gos, t_sem.at[1])
     load_go.start()
@@ -131,15 +131,22 @@
     w0 = jnp.where(c == 0, one, cw0)
     w1 = jnp.where(c == 0, one, cw1)
     spans = (slice(0, HS), slice(HS, SL))
-    pltpu.make_async_copy(gos, src, t_sem.at[0]).wait()
-    sources = []
-    for span in spans:
-        v = src[:, span].astype(F32)
-        sources += [(v * w0).astype(BF16), (v * w1).astype(BF16)]
-    slabs = dot_tn(pick[...], jnp.concatenate(sources, axis=0)).astype(BF16)
-    for e in range(NZ):
-        slab_out[0, e] = slabs[e * 16 : (e + 1) * 16]
-    slab_in[0, z] = slab_out[0, z]
+    pltpu.make_async_copy(go_hbm, src, t_sem.at[0]).wait()
+    far_first = [NZ // 2] + [d for k in range(NZ // 2 - 1, 0, -1) for d in (k, NZ - k)]
+    xorder = [x, wx(x - 1), wx(x + 1), wx(x + 2)]
+
+    def make_slabs(j):
+        sources = []
+        for h in range(2):
+            span = pl.ds(pl.multiple_of(xorder[j] * SL + h * HS, 128), HS)
+            v = src[:, span].astype(F32)
+            sources += [(v * w0).astype(BF16), (v * w1).astype(BF16)]
+        slabs = dot_tn(pick[...], jnp.concatenate(sources, axis=0)).astype(BF16)
+        for e in range(NZ):
+            slab_out[j, e] = slabs[e * 16 : (e + 1) * 16]
+        slab_in[j, z] = slab_out[j, z]
+
+    make_slabs(0)
 
     pl.semaphore_wait(barrier, len(partners))
 
@@ -155,18 +162,27 @@
         def _():
             remote(wd.at[:, own_units], wd.at[:, sib_units], p_send.at[0], p_recv.at[0], sibling).start()
 
-    def exchange_z(which, s_sem, r_sem):
-        for d in range(1, NZ):
+    def start_z(which, s_sem, r_sem):
+        for d in far_first:
             remote(
                 slab_out.at[which, lax.rem(z + d, NZ)], slab_in.at[which, z],
                 s_sem.at[d], r_sem.at[d], peers_z[d - 1],
             ).start()
-        if which == 0:
-            give_weights()
+
+    def end_z(which, r_sem):
         for d in range(1, NZ):
             arrived(slab_in.at[which, lax.rem(z - d + NZ, NZ)], r_sem.at[d])
 
-    exchange_z(0, za_s, za_r)
+    start_z(0, za_s.at[0], za_r.at[0])
+
+    @pl.when(c == 1)
+    def _():
+        for j in range(1, NX):
+            make_slabs(j)
+            start_z(j, za_s.at[j], za_r.at[j])
+
+    give_weights()
+    end_z(0, za_r.at[0])
 
     row = lax.broadcasted_iota(jnp.int32, (PIECE, NZ * 16), 0)
     col = lax.broadcasted_iota(jnp.int32, (PIECE, NZ * 16), 1)
@@ -175,10 +191,14 @@
     tidy1 = jnp.where(
         (block * CAPA + inner - CAPA == row) & (inner >= CAPA) & (inner < 2 * CAPA), 1.0, 0.0
     ).astype(BF16)
-    got = slab_in[0].reshape(NZ * 16, HS)
-    mine = c * PER + x * NY + y
-    xg[mine, :, 0:HS] = dot_nn(tidy0, got).astype(BF16)
-    xg[mine, :, HS:SL] = dot_nn(tidy1, got).astype(BF16)
+
+    def settle(j):
+        got = slab_in[j].reshape(NZ * 16, HS)
+        mine = c * PER + xorder[j] * NY + y
+        xg[mine, :, 0:HS] = dot_nn(tidy0, got).astype(BF16)
+        xg[mine, :, HS:SL] = dot_nn(tidy1, got).astype(BF16)
+
+    settle(0)
 
     halves = (pl.ds(0, HS), pl.ds(HS, HS))
     HY = NY // 2
@@ -211,9 +231,11 @@
         arrived(xg.at[p], gy.at[j, d, s])
         if s == 0 and not short:
             send(xg.at[p], gy.at[j, d, 1], ynear[d])
+        chain = j < 2 and not short
         if s == 1:
             send(xg.at[p], gy.at[j, d, 2], ynear[d])
-            send(xg.at[p, :, halves[d]], gy.at[j, d, 3], yfar[d])
+        if s == (2 if chain else 1):
+            send(xg.at[p, :, halves[d]], gy.at[j, d, 3], ynear[d] if chain else yfar[d])
         return p
 
     def gather_y_then_x():
@@ -236,20 +258,17 @@
                 arrived(xg.at[p], gx.at[k, i])
                 to_sibling(p)
 
-    def gather_x_then_y():
+    def gather_y():
         def piece_of(xx):
             return lambda yy: PER + xx * NY + yy
 
-        p = piece_of(x)(y)
-        along_x(p, 0)
-        begin_y(0, p, False)
-        to_sibling(p)
-        streams = [(0, piece_of(x))] + [(1 + k, piece_of(from_x(k))) for k in (1, 2, 0)]
-        for j, piece_at in streams[1:]:
-            p = piece_at(y)
-            arrived(xg.at[p], gx.at[j - 1, 0])
-            begin_y(j, p, False)
-            to_sibling(p)
+        streams = [(j, piece_of(xorder[j])) for j in range(NX)]
+        for j, piece_at in streams:
+            if j:
+                end_z(j, za_r.at[j])
+                settle(j)
+            begin_y(j, piece_at(y), False)
+            to_sibling(piece_at(y))
         for s in range(HY):
             for j, piece_at in streams:
                 for d in range(2):
@@ -258,17 +277,29 @@
                         to_sibling(p)
 
     pl.when(c == 0)(gather_y_then_x)
-    pl.when(c == 1)(gather_x_then_y)
-    arrived(xg.at[pl.ds((1 - c) * PER, PER)], d_recv)
+    pl.when(c == 1)(gather_y)
 
     def rows_of(a, i):
         return xg[a * PER + i * NY : a * PER + (i + 1) * NY].reshape(ROWS, SL)
 
-    pre = dot_nn(rows_of(0, 0), wgu[0, :, own_pair])
-    d_hidden = dot_nt(rows_of(1, 0), wd[0, own_units])
-    for i in range(1, NX):
-        pre = pre + dot_nn(rows_of(0, i), wgu[i, :, own_pair])
-        d_hidden = d_hidden + dot_nt(rows_of(1, i), wd[i, own_units])
+    def products(which):
+        if which == 0:
+            v = dot_nn(rows_of(0, 0), wgu[0, :, own_pair])
+            for i in range(1, NX):
+                v = v + dot_nn(rows_of(0, i), wgu[i, :, own_pair])
+            pre_ref[...] = v
+        else:
+            v = dot_nt(rows_of(1, 0), wd[0, own_units])
+            for i in range(1, NX):
+                v = v + dot_nt(rows_of(1, i), wd[i, own_units])
+            dh_ref[...] = v
+
+    for when, which in ((0, 0), (1, 1)):
+        pl.when(c == when)(functools.partial(products, which))
+    arrived(xg.at[pl.ds((1 - c) * PER, PER)], d_recv)
+    for when, which in ((0, 1), (1, 0)):
+        pl.when(c == when)(functools.partial(products, which))
+    pre, d_hidden = pre_ref[...], dh_ref[...]
     gate_pre, up_pre = pre[:, :HID], pre[:, HID:]
     sigma = jax.nn.sigmoid(gate_pre)
     silu = gate_pre * sigma
@@ -355,6 +386,7 @@
     c_short = [False]
     back_order = (3, -3, HY, 2, -2, 1, -1, 0)
     chunk_of = (0, 1, 3)
+    chunk_order = chunk_of + (2,)
 
     def at_y(off):
         return wy(y + off)
@@ -372,7 +404,7 @@
     def begin_y_then_x():
         arrived(wgu.at[:, :, sib_pair], p_recv.at[0])
         arrived(dgu.at[:, sib_pair], p_recv.at[1])
-        for j in range(NX):
+        for j in chunk_order:
             input_grad_chunk(j)
             y_first(j, lambda off: own(wx(x + 2 - j) * NY + at_y(off)))
 
@@ -404,13 +436,13 @@
         def get(j):
             return lambda off: own(wx(x + 2 - j) * NY + at_y(off))
 
-        for j in range(NX):
+        for j in chunk_order:
             for d in range(2):
                 y_second(j, d, get(j))
-        for j in range(NX):
+        for j in chunk_order:
             for d in range(2):
                 y_out(j, d, 0, get(j)(1 - 2 * d) + y_came(j, d, 1))
-        for j in range(NX):
+        for j in chunk_order:
             v = get(j)(0) + y_came(j, 0, 0) + y_came(j, 1, 0)
             if j in chunk_of:
                 x_out(chunk_of.index(j), 0, v)
@@ -424,10 +456,11 @@
     done = res[x].astype(BF16)
     back = (dot_tn(tidy0, done[:, :HS]) + dot_tn(tidy1, done[:, HS:])).astype(BF16)
     for e in range(NZ):
-        slab_out[1, e] = back[e * 16 : (e + 1) * 16]
-    slab_in[1, z] = slab_out[1, z]
-    exchange_z(1, zb_s, zb_r)
-    chosen = dot_nn(pick[...], slab_in[1].reshape(NZ * 16, HS))
+        slab_out[NX, e] = back[e * 16 : (e + 1) * 16]
+    slab_in[NX, z] = slab_out[NX, z]
+    start_z(NX, zb_s, zb_r)
+    end_z(NX, zb_r)
+    chosen = dot_nn(pick[...], slab_in[NX].reshape(NZ * 16, HS))
     c0 = jnp.where(c == 0, cw0, one)
     c1 = jnp.where(c == 0, cw1, one)
     scores = [jnp.zeros((TOKB, 1), F32), jnp.zeros((TOKB, 1), F32)]
@@ -442,7 +475,7 @@
     lane = lax.broadcasted_iota(jnp.int32, (TOKB, 128), 1)
     fsc[tp] = jnp.where(lane == 0, scores[0], jnp.where(lane == 1, scores[1], 0.0))
 
-    for d in range(1, NT):
+    for d in [NT // 2] + [d for k in range(NT // 2 - 1, 0, -1) for d in (k, NT - k)]:
         remote(fin.at[tp], fin.at[tp], f_s.at[0, d], f_r.at[0, d], peers_t[d - 1]).start()
         remote(fsc.at[tp], fsc.at[tp], f_s.at[1, d], f_r.at[1, d], peers_t[d - 1]).start()
     for d in range(1, NT):
@@ -459,12 +492,11 @@
         gcomb_ref[k : k + 1, :] = jnp.sum(jnp.where(diagonal, total_score[:, k : k + 1], 0.0), axis=0, keepdims=True)
 
     for d in range(1, NZ):
-        sent(slab_out.at[0, 0], za_s.at[d])
-        sent(slab_out.at[1, 0], zb_s.at[d])
+        sent(slab_out.at[0, 0], za_s.at[0, d])
+        sent(slab_out.at[0, 0], zb_s.at[d])
     for d in range(1, NT):
         sent(fin.at[tp], f_s.at[0, d])
         sent(fsc.at[tp], f_s.at[1, d])
-    sent(xg.at[pl.ds(0, PER - 1)], g_send)
     sent(xg.at[pl.ds(c * PER, PER)], d_send)
 
     def y_sent(j):
@@ -475,6 +507,7 @@
 
     @pl.when(c == 0)
     def _():
+        sent(xg.at[pl.ds(0, PER - 1)], g_send)
         sent(wgu.at[:, :, own_pair], p_send.at[0])
         sent(dgu.at[:, own_pair], p_send.at[1])
         for k in range(NX - 1):
@@ -484,6 +517,10 @@
 
     @pl.when(c == 1)
     def _():
+        sent(xg.at[pl.ds(0, PER - NX)], g_send)
+        for j in range(1, NX):
+            for d in range(1, NZ):
+                sent(slab_out.at[0, 0], za_s.at[j, d])
         sent(wd.at[:, own_units], p_send.at[0])
         sent(hid.at[:, own_units], p_send.at[1])
         for k in range(NX - 1):
@@ -534,18 +571,19 @@
                 vmem((NX, 2, half_y, piece, sl), BF16),
                 vmem((NX, 2, half_y, piece, sl), BF16),
                 vmem((NX, piece, sl), F32),
-                vmem((2, NZ, 16, hs), BF16),
-                vmem((2, NZ, 16, hs), BF16),
+                vmem((NX + 1, NZ, 16, hs), BF16),
+                vmem((NX + 1, NZ, 16, hs), BF16),
                 vmem((NT, tokb, sl), BF16),
                 vmem((NT, tokb, 128), F32),
                 vmem((4 * tokb, NZ * 16), BF16),
-                vmem((tokb, sl), BF16), vmem((tokb, sl), BF16),
+                vmem((tokb, d), BF16), vmem((tokb, sl), BF16),
                 vmem((NX, sl, 4 * hidden), BF16),
                 vmem((NX, 2 * hidden, sl), BF16),
                 vmem((rows, 2 * hidden), BF16),
                 vmem((rows, 4 * hidden), BF16),
+                vmem((rows, 2 * hidden), F32), vmem((rows, hidden), F32),
                 dma((3 * NX,)), dma((2,)),
-                dma((NZ,)), dma((NZ,)), dma((NZ,)), dma((NZ,)),
+                dma((NX, NZ)), dma((NX, NZ)), dma((NZ,)), dma((NZ,)),
                 dma((NX - 1, NY)), dma((NX, 2, half_y)),
                 dma(()), dma(()), dma(()),
                 dma((2,)), dma((2,)),

time: 80.6 us -> 80.1 us (level)
  no operation moved by 1% of the time
where the time goes in v4:
time: 80.1 us; the launch traced here: 80 us
  Pallas kernels  79.3 us (99%)
    pallas_call x1, Pallas kernels, step(): pl.pallas_call(functools.partial(kernel, (NX, NY, NZ, cap)), out_shape=(v...  77.8 us

profile of v4, /device:TPU:1, one launch (start us, length us, event | category | flops | bytes accessed | tf_op | source)
XLA Modules:
  0.0 80.0 jit_solution(3688306560756822781)
XLA Ops:
  0.6 77.8 %shard_map.118 = (bf16[16,3072]{1,0:T(8,128)(2,1)S(1)}, bf16[16,3072]{1,0:T(8,128)(2,1)S(1)}, f32[2,16]{1,0:T(2,128)S(1)}, bf16[3072,128]{1,0:T(8,128)(2,1)S(1)}...) custom-call(s32[2,16]{1,0:T(2,128)} %bitcast.3, f32[2,16]{1,0:T(2,128)} %bitcast.4, ...), custom_call_target="tpu_custom_call" | custom-call | tf_op jit(solution)/shard_map/pallas_call | solution.py:554
  78.5 1.5 %shard_map.119 = (bf16[3072,128]{1,0:T(8,128)(2,1)}, bf16[3072,128]{1,0:T(8,128)(2,1)}, bf16[128,3072]{1,0:T(8,128)(2,1)}, bf16[16,3072]{1,0:T(8,128)(2,1)}, bf16[16,3072]{1,0:T(8,128)(2,1)}, /*index=5*/f32[2,16]{1,0:T(2,128)}) custom-call(bf16[3072,128]{1,0:T(8,128)(2,1)S(1)} %get-tuple-element.18.refs_0_, bf16[3072,128]{1,0:T(8,128)(2,1)S(1)} %get-tuple-element.19.refs_1_, ...), custom_call_target="tpu_custom_call" | custom-call | tf_op jit(solution)/shard_map/pallas_call | solution.py:599

commit v5 on v4

--- a/solution.py
+++ b/solution.py
@@ -270,14 +270,17 @@
             begin_y(j, piece_at(y), False)
             to_sibling(piece_at(y))
         for s in range(HY):
+            if s == HY - 1:
+                arrived(xg.at[pl.ds(0, PER)], d_recv)
+                products(0)
+                make_hidden()
+                remote(hid.at[:, own_units], hid.at[:, sib_units], p_send.at[1], p_recv.at[1], sibling).start()
             for j, piece_at in streams:
                 for d in range(2):
                     p = onward_y(j, d, s, piece_at, False)
                     if s < HY - 1 or d == 1:
                         to_sibling(p)
 
-    pl.when(c == 0)(gather_y_then_x)
-    pl.when(c == 1)(gather_y)
 
     def rows_of(a, i):
         return xg[a * PER + i * NY : a * PER + (i + 1) * NY].reshape(ROWS, SL)
@@ -294,26 +297,15 @@
                 v = v + dot_nt(rows_of(1, i), wd[i, own_units])
             dh_ref[...] = v
 
-    for when, which in ((0, 0), (1, 1)):
-        pl.when(c == when)(functools.partial(products, which))
-    arrived(xg.at[pl.ds((1 - c) * PER, PER)], d_recv)
-    for when, which in ((0, 1), (1, 0)):
-        pl.when(c == when)(functools.partial(products, which))
-    pre, d_hidden = pre_ref[...], dh_ref[...]
-    gate_pre, up_pre = pre[:, :HID], pre[:, HID:]
-    sigma = jax.nn.sigmoid(gate_pre)
-    silu = gate_pre * sigma
-    hid[:, own_units] = (silu * up_pre).astype(BF16)
-    dgu[:, pl.ds(0, HID)] = (d_hidden * up_pre * sigma * (1.0 + gate_pre * (1.0 - sigma))).astype(BF16)
-    dgu[:, pl.ds(HID, HID)] = (d_hidden * silu).astype(BF16)
-
-    @pl.when(c == 0)
-    def _():
-        remote(dgu.at[:, own_pair], dgu.at[:, sib_pair], p_send.at[1], p_recv.at[1], sibling).start()
-
-    @pl.when(c == 1)
-    def _():
-        remote(hid.at[:, own_units], hid.at[:, sib_units], p_send.at[1], p_recv.at[1], sibling).start()
+    def make_hidden():
+        gate_pre, up_pre = pre_ref[:, :HID], pre_ref[:, HID:]
+        hid[:, own_units] = (gate_pre * jax.nn.sigmoid(gate_pre) * up_pre).astype(BF16)
+
+    def make_grads():
+        gate_pre, up_pre, d_hidden = pre_ref[:, :HID], pre_ref[:, HID:], dh_ref[...]
+        sigma = jax.nn.sigmoid(gate_pre)
+        dgu[:, pl.ds(0, HID)] = (d_hidden * up_pre * sigma * (1.0 + gate_pre * (1.0 - sigma))).astype(BF16)
+        dgu[:, pl.ds(HID, HID)] = (d_hidden * (gate_pre * sigma)).astype(BF16)
 
     def weight_grads(first, last):
         def step(i, carry):
@@ -328,8 +320,6 @@
 
         lax.fori_loop(first, last, step, 0)
 
-    weight_grads(0, NX // 2)
-
     def expert_out_chunk(j):
         xx = wx(x + 2 - j)
         part[pl.ds(xx * NY, NY)] = dot_nn(hid[...], wd[xx]).reshape(NY, PIECE, SL)
@@ -408,7 +398,24 @@
             input_grad_chunk(j)
             y_first(j, lambda off: own(wx(x + 2 - j) * NY + at_y(off)))
 
-    pl.when(c == 0)(begin_x_then_y)
+    @pl.when(c == 0)
+    def _():
+        gather_y_then_x()
+        products(0)
+        make_hidden()
+        begin_x_then_y()
+        arrived(xg.at[pl.ds(PER, PER)], d_recv)
+        products(1)
+        make_grads()
+        remote(dgu.at[:, own_pair], dgu.at[:, sib_pair], p_send.at[1], p_recv.at[1], sibling).start()
+
+    @pl.when(c == 1)
+    def _():
+        gather_y()
+        products(1)
+        make_grads()
+
+    weight_grads(0, NX // 2)
     pl.when(c == 1)(begin_y_then_x)
 
     weight_grads(NX // 2, NX)

time: 80.1 us -> 84.7 us (1.057)
  Pallas kernels: 79.3 us -> 83.9 us
    pallas_call x1, Pallas kernels: 77.8 us -> 82.4 us  [step(): pl.pallas_call(functools.partial(kernel, (NX, NY, NZ, cap)), out_shape=(v...]
where the time goes in v5:
time: 84.7 us; the launch traced here: 84.5 us
  Pallas kernels  83.9 us (99%)
    pallas_call x1, Pallas kernels, step(): pl.pallas_call(functools.partial(kernel, (NX, NY, NZ, cap)), out_shape=(v...  82.4 us

profile of v5, /device:TPU:1, one launch (start us, length us, event | category | flops | bytes accessed | tf_op | source)
XLA Modules:
  0.0 84.5 jit_solution(11475424501470064034)
XLA Ops:
  0.6 82.4 %shard_map.118 = (bf16[16,3072]{1,0:T(8,128)(2,1)S(1)}, bf16[16,3072]{1,0:T(8,128)(2,1)S(1)}, f32[2,16]{1,0:T(2,128)S(1)}, bf16[3072,128]{1,0:T(8,128)(2,1)S(1)}...) custom-call(s32[2,16]{1,0:T(2,128)} %bitcast.3, f32[2,16]{1,0:T(2,128)} %bitcast.4, ...), custom_call_target="tpu_custom_call" | custom-call | tf_op jit(solution)/shard_map/pallas_call | solution.py:561
  83.0 1.5 %shard_map.119 = (bf16[3072,128]{1,0:T(8,128)(2,1)}, bf16[3072,128]{1,0:T(8,128)(2,1)}, bf16[128,3072]{1,0:T(8,128)(2,1)}, bf16[16,3072]{1,0:T(8,128)(2,1)}, bf16[16,3072]{1,0:T(8,128)(2,1)}, /*index=5*/f32[2,16]{1,0:T(2,128)}) custom-call(bf16[3072,128]{1,0:T(8,128)(2,1)S(1)} %get-tuple-element.18.refs_0_, bf16[3072,128]{1,0:T(8,128)(2,1)S(1)} %get-tuple-element.19.refs_1_, ...), custom_call_target="tpu_custom_call" | custom-call | tf_op jit(solution)/shard_map/pallas_call | solution.py:606

commit v6 on v4

--- a/solution.py
+++ b/solution.py
@@ -203,6 +203,7 @@
     halves = (pl.ds(0, HS), pl.ds(HS, HS))
     HY = NY // 2
     order = (0, -1, 1, -2, 2, -3, 3, HY)
+    RELAYED = 5
 
     def to_sibling(p):
         remote(xg.at[p], xg.at[p], d_send, d_recv, sibling).start()
@@ -211,8 +212,15 @@
         remote(ref, ref, g_send, sem, device).start()
 
     def along_x(p, i):
-        for k in range(NX - 1):
+        for k in range(1 if i < RELAYED else 0, NX - 1):
             send(xg.at[p], gx.at[k, i], xdev[k])
+
+    def relay_x(i):
+        for d, k in enumerate((1, 2)):
+            p = from_x(k) * NY + wy(y + order[i])
+            arrived(xg.at[p], gx.at[k, i])
+            send(xg.at[p, :, halves[d]], gx.at[(0, NX - 1)[d], i], xdev[k])
+            to_sibling(p)
 
     def from_x(k):
         return wx(x - (2, 1, -1)[k])
@@ -252,7 +260,15 @@
                 if s < HY - 1 or d == 1:
                     along_x(p, 2 * s + 1 if s == HY - 1 else 2 * s + 1 + d)
                     to_sibling(p)
+            for i in ((), (0,), (1, 2), (3, 4))[s]:
+                relay_x(i)
         for i in range(NY):
+            if i < RELAYED:
+                p = from_x(0) * NY + wy(y + order[i])
+                for d in range(2):
+                    arrived(xg.at[p, :, halves[d]], gx.at[(0, NX - 1)[d], i])
+                to_sibling(p)
+                continue
             for k in range(NX - 1):
                 p = from_x(k) * NY + wy(y + order[i])
                 arrived(xg.at[p], gx.at[k, i])
@@ -584,7 +600,7 @@
                 vmem((rows, 2 * hidden), F32), vmem((rows, hidden), F32),
                 dma((3 * NX,)), dma((2,)),
                 dma((NX, NZ)), dma((NX, NZ)), dma((NZ,)), dma((NZ,)),
-                dma((NX - 1, NY)), dma((NX, 2, half_y)),
+                dma((NX, NY)), dma((NX, 2, half_y)),
                 dma(()), dma(()), dma(()),
                 dma((2,)), dma((2,)),
                 dma((NX - 1, NY)), dma((NX - 1, NY)),

time: 80.1 us -> 81.3 us (1.015)
  Pallas kernels: 79.3 us -> 80.5 us
    pallas_call x1, Pallas kernels: 77.8 us -> 79 us  [step(): pl.pallas_call(functools.partial(kernel, (NX, NY, NZ, cap)), out_shape=(v...]
where the time goes in v6:
time: 81.3 us; the launch traced here: 81.1 us
  Pallas kernels  80.5 us (99%)
    pallas_call x1, Pallas kernels, step(): pl.pallas_call(functools.partial(kernel, (NX, NY, NZ, cap)), out_shape=(v...  79 us

profile of v6, /device:TPU:1, one launch (start us, length us, event | category | flops | bytes accessed | tf_op | source)
XLA Modules:
  0.0 81.1 jit_solution(16067443781215413307)
XLA Ops:
  0.6 79.0 %shard_map.118 = (bf16[16,3072]{1,0:T(8,128)(2,1)S(1)}, bf16[16,3072]{1,0:T(8,128)(2,1)S(1)}, f32[2,16]{1,0:T(2,128)S(1)}, bf16[3072,128]{1,0:T(8,128)(2,1)S(1)}...) custom-call(s32[2,16]{1,0:T(2,128)} %bitcast.3, f32[2,16]{1,0:T(2,128)} %bitcast.4, ...), custom_call_target="tpu_custom_call" | custom-call | tf_op jit(solution)/shard_map/pallas_call | solution.py:570
  79.6 1.5 %shard_map.119 = (bf16[3072,128]{1,0:T(8,128)(2,1)}, bf16[3072,128]{1,0:T(8,128)(2,1)}, bf16[128,3072]{1,0:T(8,128)(2,1)}, bf16[16,3072]{1,0:T(8,128)(2,1)}, bf16[16,3072]{1,0:T(8,128)(2,1)}, /*index=5*/f32[2,16]{1,0:T(2,128)}) custom-call(bf16[3072,128]{1,0:T(8,128)(2,1)S(1)} %get-tuple-element.18.refs_0_, bf16[3072,128]{1,0:T(8,128)(2,1)S(1)} %get-tuple-element.19.refs_1_, ...), custom_call_target="tpu_custom_call" | custom-call | tf_op jit(solution)/shard_map/pallas_call | solution.py:615

commit v7 on v4

--- a/solution.py
+++ b/solution.py
@@ -231,7 +231,7 @@
         arrived(xg.at[p], gy.at[j, d, s])
         if s == 0 and not short:
             send(xg.at[p], gy.at[j, d, 1], ynear[d])
-        chain = j < 2 and not short
+        chain = not short
         if s == 1:
             send(xg.at[p], gy.at[j, d, 2], ynear[d])
         if s == (2 if chain else 1):

time: 80.1 us -> 80.1 us (level)
  no operation moved by 1% of the time
where the time goes in v7:
time: 80.1 us; the launch traced here: 80 us
  Pallas kernels  79.3 us (99%)
    pallas_call x1, Pallas kernels, step(): pl.pallas_call(functools.partial(kernel, (NX, NY, NZ, cap)), out_shape=(v...  77.8 us

profile of v7, /device:TPU:1, one launch (start us, length us, event | category | flops | bytes accessed | tf_op | source)
XLA Modules:
  0.0 80.0 jit_solution(7945330100336583436)
XLA Ops:
  0.6 77.8 %shard_map.118 = (bf16[16,3072]{1,0:T(8,128)(2,1)S(1)}, bf16[16,3072]{1,0:T(8,128)(2,1)S(1)}, f32[2,16]{1,0:T(2,128)S(1)}, bf16[3072,128]{1,0:T(8,128)(2,1)S(1)}...) custom-call(s32[2,16]{1,0:T(2,128)} %bitcast.3, f32[2,16]{1,0:T(2,128)} %bitcast.4, ...), custom_call_target="tpu_custom_call" | custom-call | tf_op jit(solution)/shard_map/pallas_call | solution.py:554
  78.5 1.5 %shard_map.119 = (bf16[3072,128]{1,0:T(8,128)(2,1)}, bf16[3072,128]{1,0:T(8,128)(2,1)}, bf16[128,3072]{1,0:T(8,128)(2,1)}, bf16[16,3072]{1,0:T(8,128)(2,1)}, bf16[16,3072]{1,0:T(8,128)(2,1)}, /*index=5*/f32[2,16]{1,0:T(2,128)}) custom-call(bf16[3072,128]{1,0:T(8,128)(2,1)S(1)} %get-tuple-element.18.refs_0_, bf16[3072,128]{1,0:T(8,128)(2,1)S(1)} %get-tuple-element.19.refs_1_, ...), custom_call_target="tpu_custom_call" | custom-call | tf_op jit(solution)/shard_map/pallas_call | solution.py:599
